TPU v7x, 32 devices: a whole 2x2x4 slice. The times are simulated.
32 devices in a mesh: gx: 8 (over z, x), gy: 4 (over y, core).
Axes of the slice: x: 2, y: 2, z: 4, core: 2. Of those that a mesh axis runs over, the one named last changes fastest.
Arguments:
- features: bfloat16 [256, 512, 128], P(('gx', 'gy')), may hold values from -6 to 6
- weights: bfloat16 [27, 128, 128], replicated, may hold values from -0.109375 to 0.109375
- cotangent: bfloat16 [256, 512, 128], P(('gx', 'gy')), may hold values from -6 to 6
- occupancy: int32 [256, 512], P(('gx', 'gy')), may hold values 0 or 1
- slot_pos: int32 [256], P(('gx', 'gy')), may hold values from -1 to 15, as said below
Outputs:
- outputs: bfloat16 [256, 512, 128], P(('gx', 'gy'))
- grad_input: bfloat16 [256, 512, 128], P(('gx', 'gy'))
- grad_weight: float32 [27, 128, 128], replicated
Inputs may be any that keep to these rules, and one draw needn't show every extreme that they name: `slot_pos`: on each device the 8 slots name distinct positions of its region; live slots come first and the rest hold -1; each device has at least 4 live slots, and some device has all 8 live.
All inputs are finite; a program needn't handle non-finite values. No bound on the sum of `occupancy` on one device may be relied on, other than what follows from the above.
Results may differ from a plain program's by a relative error of at most 0.001.
Values may be sent and summed in bfloat16 or wider, within the bound.
A program may use at most 64 MiB of HBM per device.

v0:
```python
import math

import jax
import jax.numpy as jnp
from jax import lax
from jax.sharding import PartitionSpec as P

BRICK = 8
REGION_X = 4
REGION_Y = 2
REGION_Z = 2


def with_halo(value, sides, width):
    for axis, dim in sides:
        size, length = (lax.axis_size(axis), value.shape[dim])
        up = [(i, (i + 1) % size) for i in range(size - 1)]
        down = [(j, i) for i, j in up]
        last = lax.slice_in_dim(value, length - width, length, axis=dim)
        leading = lax.slice_in_dim(value, 0, width, axis=dim)
        before = lax.ppermute(last, axis, up)
        after = lax.ppermute(leading, axis, down)
        value = jnp.concatenate([before, value, after], axis=dim)
    return value


def offset_list():
    result = []
    for along_x in (-1, 0, 1):
        for along_y in (-1, 0, 1):
            for along_z in (-1, 0, 1):
                result.append((along_x, along_y, along_z))
    return result


def brick_patches(padded, corner, first_offset, offset_count):
    channels = padded.shape[-1]
    block_span = BRICK + 2
    starts = (corner[0], corner[1], corner[2], jnp.zeros((), jnp.int32))
    block = lax.dynamic_slice(padded, starts, (block_span, block_span, block_span, channels))
    columns = []
    for along_x, along_y, along_z in offset_list()[first_offset : first_offset + offset_count]:
        window_cells = block[
            along_x + 1 : along_x + 1 + BRICK,
            along_y + 1 : along_y + 1 + BRICK,
            along_z + 1 : along_z + 1 + BRICK,
        ]
        columns.append(window_cells.reshape(BRICK**3, channels))
    return jnp.concatenate(columns, axis=1)


def shards(features, weights, cotangent, occupancy, slot_pos):
    slot_count, voxels, channels = features.shape
    positions = REGION_X * REGION_Y * REGION_Z
    active = (occupancy == 1) & (slot_pos >= 0)[:, None]
    zero_value = jnp.zeros((), features.dtype)
    masked_in = jnp.where(active[:, :, None], features, zero_value)
    masked_cot = jnp.where(active[:, :, None], cotangent, zero_value)
    one_hot = (jnp.arange(positions, dtype=jnp.int32)[:, None] == slot_pos[None, :]).astype(
        jnp.bfloat16
    )
    w_forward = weights.reshape(27 * channels, channels)
    w_backward = weights[::-1].transpose(0, 2, 1).reshape(27 * channels, channels)

    def local_grid(values):
        placed = jnp.dot(
            one_hot,
            values.reshape(slot_count, voxels * channels),
            preferred_element_type=jnp.float32,
        ).astype(jnp.bfloat16)
        voxel_cells = placed.reshape(REGION_X, REGION_Y, REGION_Z, BRICK, BRICK, BRICK, channels)
        voxel_cells = voxel_cells.transpose(0, 3, 1, 4, 2, 5, 6).reshape(
            REGION_X * BRICK, REGION_Y * BRICK, REGION_Z * BRICK, channels
        )
        padded = with_halo(voxel_cells, (("gx", 0), ("gy", 1)), 1)
        return jnp.pad(padded, ((0, 0), (0, 0), (1, 1), (0, 0)))

    def brick_corner(slot_index):
        position = jnp.maximum(slot_pos[slot_index], 0)
        return (
            position // (REGION_Y * REGION_Z) * BRICK,
            position // REGION_Z % REGION_Y * BRICK,
            position % REGION_Z * BRICK,
        )

    grid_x = local_grid(masked_in)
    slot_ids = jnp.arange(slot_count, dtype=jnp.int32)
    devices = lax.axis_size("gx") * lax.axis_size("gy")
    scale = 1.0 / math.sqrt(float(devices * slot_count * voxels))

    def make_forward():

        def forward_step(running, slot_index):
            patches = brick_patches(grid_x, brick_corner(slot_index), 0, 27)
            total = jnp.dot(patches, w_forward, preferred_element_type=jnp.float32)
            keep_mask = active[slot_index].astype(jnp.float32)[:, None]
            result = (total * keep_mask).astype(jnp.bfloat16)
            terms = jnp.einsum(
                "vk,vc->kc", patches, masked_cot[slot_index], preferred_element_type=jnp.float32
            )
            running = running + terms.reshape(27, channels, channels)
            return (running, result)

        return forward_step

    local_grad, outputs = lax.scan(
        make_forward(), jnp.zeros((27, channels, channels), jnp.float32), slot_ids
    )
    grad_weight = lax.psum(local_grad, ("gx", "gy")) * scale
    grid_dy = local_grid(masked_cot)

    def backward_step(running, slot_index):
        patches = brick_patches(grid_dy, brick_corner(slot_index), 0, 27)
        total = jnp.dot(patches, w_backward, preferred_element_type=jnp.float32)
        keep_mask = active[slot_index].astype(jnp.float32)[:, None]
        return (running, (total * keep_mask).astype(jnp.bfloat16))

    unused, grad_input = lax.scan(backward_step, jnp.zeros((), jnp.float32), slot_ids)
    return (outputs, grad_input, grad_weight)


def solution(mesh):
    return jax.shard_map(
        shards,
        mesh=mesh,
        in_specs=(
            P(("gx", "gy"), None, None),
            P(),
            P(("gx", "gy"), None, None),
            P(("gx", "gy"), None),
            P(("gx", "gy")),
        ),
        out_specs=(P(("gx", "gy"), None, None), P(("gx", "gy"), None, None), P()),
        check_vma=False,
    )
```

profile of v0, /device:TPU:0, one launch (start us, length us, event | category | flops | bytes accessed | tf_op | source)
XLA Modules:
  0.0 388.4 jit_solution(13651319076992484567)
XLA Ops:
  8.7 2.8 broadcast_select_fusion
  14.4 5.5 %collective-permute-start = (bf16[1,16,16,128]{3,2,1,0:T(8,128)(2,1)S(1)}, bf16[1,16,16,128]{3,2,1,0:T(8,128)(2,1)S(1)}, u32[]{:S(2)}, u32[]{:S(2)}) collective-permute-start(bf16[1,16,16,128]{3,2,1,0:T(8,128)(2,1)S(1)} %get-tuple-element.399), channel_id=1, source_target_pairs={{0,4},{4,8},{8,12},{12,16},{16,20},{20,24},{24,28},{1,5},{5,9},{9,... | collective-permute-start | bytes 196616 | tf_op jit(solution)/shard_map/ppermute | solution.py:21
  23.5 5.4 %collective-permute-start.4 = (bf16[1,16,16,128]{3,2,1,0:T(8,128)(2,1)}, bf16[1,16,16,128]{3,2,1,0:T(8,128)(2,1)S(1)}, u32[]{:S(2)}, u32[]{:S(2)}) collective-permute-start(bf16[1,16,16,128]{3,2,1,0:T(8,128)(2,1)} %get-tuple-element.397), channel_id=1, source_target_pairs={{0,4},{4,8},{8,12},{12,16},{16,20},{20,24},{24,28},{1,5},{5,9},{9,... | collective-permute-start | bytes 196616 | tf_op jit(solution)/shard_map/ppermute | solution.py:21
  31.0 3.7 collective-permute-start.2
  38.6 3.7 collective-permute-start.6
  42.3 5.6 %select_maximum_fusion.4 = bf16[34,18,18,128]{3,2,1,0:T(8,128)(2,1)} fusion(bf16[34,1,16,128]{3,2,1,0:T(8,128)(2,1)S(1)} %collective-permute-done.3, bf16[34,1,16,128]{3,2,1,0:T(8,128)(2,1)} %collective-permute-done.2, bf16[1,16,16,128]{3,2,1,0:T(8,128)(2,1)S(1)} %collective-permute-done.1, bf16[32,16,16,128]{3,2,1,0:T(8,128)(2,1)S(1)} %bitcast.277, ...), kind=kLoop, calls=%fused_computation.131 | loop fusion | flops 25380864 | bytes 5326848 | tf_op jit(solution)/shard_map/concatenate | solution.py:23
  49.0 192.9 %while.30 = (s32[]{:T(128)}, f32[27,128,128]{2,1,0:T(8,128)}, bf16[8,512,128]{2,1,0:T(8,128)(2,1)}, s32[8]{0:T(128)S(1)}, s32[8]{0:T(128)S(1)}, /*index=5*/bf16[...) while((s32[]{:T(128)}, f32[27,128,128]{2,1,0:T(8,128)}, ...), condition=%wide.region_1.2_spmd.clone, body=%wide.region_0.1_spmd.clone.sunk | while | flops 906986048 | bytes 64853388 | solution.py:106
  53.1 7.2 %constant_dynamic-slice_fusion.57 = (bf16[8,8,8,128]{3,2,1,0:T(8,128)(2,1)S(1)}, bf16[8,8,8,128]{3,2,1,0:T(8,128)(2,1)S(1)}, bf16[8,8,8,128]{3,2,1,0:T(8,128)(2,...) fusion(bf16[34,18,18,128]{3,2,1,0:T(8,128)(2,1)} %get-tuple-ele, ...), kind=kLoop, calls=%fused_computation.121.clone.1 | loop fusion | bytes 7077924 | tf_op jit(solution)/shard_map/while/body/eval_jaxpr/slice | solution.py:43
  61.4 1.8 copy-done
  63.2 4.4 %copy.28 = bf16[3456,512]{1,0:T(8,128)(2,1)S(1)} copy(bf16[3456,512]{0,1:T(8,128)(2,1)} %bitcast.271) | data formatting | bytes 7077888 | tf_op jit(solution)/shard_map/while/body/eval_jaxpr/vk,vc->kc/dot_general | solution.py:98
  67.6 3.4 select_add_fusion.2
  76.8 8.1 %constant_dynamic-slice_fusion.57 = (bf16[8,8,8,128]{3,2,1,0:T(8,128)(2,1)S(1)}, bf16[8,8,8,128]{3,2,1,0:T(8,128)(2,1)S(1)}, bf16[8,8,8,128]{3,2,1,0:T(8,128)(2,...) fusion(bf16[34,18,18,128]{3,2,1,0:T(8,128)(2,1)} %get-tuple-ele, ...), kind=kLoop, calls=%fused_computation.121.clone.1 | loop fusion | bytes 7077924 | tf_op jit(solution)/shard_map/while/body/eval_jaxpr/slice | solution.py:43
  86.1 1.8 copy-done
  87.9 4.4 %copy.28 = bf16[3456,512]{1,0:T(8,128)(2,1)S(1)} copy(bf16[3456,512]{0,1:T(8,128)(2,1)} %bitcast.271) | data formatting | bytes 7077888 | tf_op jit(solution)/shard_map/while/body/eval_jaxpr/vk,vc->kc/dot_general | solution.py:98
  92.3 4.0 %select_add_fusion.2 = f32[27,128,128]{2,1,0:T(8,128)} fusion(f32[27,128,128]{2,1,0:T(8,128)} %get-tuple-element.632, bf16[27,128,512]{2,1,0:T(8,128)(2,1)S(1)} %bitcast.270, pred[]{:T(512)S(6)} %compare.85, bf16[8,512,128]{2,1,0:T(8,128)(2,1)} %get-tuple-element.659, s32[]{:T(128)S(6)} %select_n.170), kind=kOutput, calls=%fused_computation.59.clone.1 | convolution fusion | flops 453869568 | bytes 7208965 | tf_op jit(solution)/shard_map/while/body/eval_jaxpr/vk,vc->kc/dot_general | solution.py:98
  102.1 7.0 %constant_dynamic-slice_fusion.57 = (bf16[8,8,8,128]{3,2,1,0:T(8,128)(2,1)S(1)}, bf16[8,8,8,128]{3,2,1,0:T(8,128)(2,1)S(1)}, bf16[8,8,8,128]{3,2,1,0:T(8,128)(2,...) fusion(bf16[34,18,18,128]{3,2,1,0:T(8,128)(2,1)} %get-tuple-ele, ...), kind=kLoop, calls=%fused_computation.121.clone.1 | loop fusion | bytes 7077924 | tf_op jit(solution)/shard_map/while/body/eval_jaxpr/slice | solution.py:43
  110.2 1.8 copy-done
  112.0 4.4 %copy.28 = bf16[3456,512]{1,0:T(8,128)(2,1)S(1)} copy(bf16[3456,512]{0,1:T(8,128)(2,1)} %bitcast.271) | data formatting | bytes 7077888 | tf_op jit(solution)/shard_map/while/body/eval_jaxpr/vk,vc->kc/dot_general | solution.py:98
  116.4 4.0 %select_add_fusion.2 = f32[27,128,128]{2,1,0:T(8,128)} fusion(f32[27,128,128]{2,1,0:T(8,128)} %get-tuple-element.632, bf16[27,128,512]{2,1,0:T(8,128)(2,1)S(1)} %bitcast.270, pred[]{:T(512)S(6)} %compare.85, bf16[8,512,128]{2,1,0:T(8,128)(2,1)} %get-tuple-element.659, s32[]{:T(128)S(6)} %select_n.170), kind=kOutput, calls=%fused_computation.59.clone.1 | convolution fusion | flops 453869568 | bytes 7208965 | tf_op jit(solution)/shard_map/while/body/eval_jaxpr/vk,vc->kc/dot_general | solution.py:98
  126.2 6.7 %constant_dynamic-slice_fusion.57 = (bf16[8,8,8,128]{3,2,1,0:T(8,128)(2,1)S(1)}, bf16[8,8,8,128]{3,2,1,0:T(8,128)(2,1)S(1)}, bf16[8,8,8,128]{3,2,1,0:T(8,128)(2,...) fusion(bf16[34,18,18,128]{3,2,1,0:T(8,128)(2,1)} %get-tuple-ele, ...), kind=kLoop, calls=%fused_computation.121.clone.1 | loop fusion | bytes 7077924 | tf_op jit(solution)/shard_map/while/body/eval_jaxpr/slice | solution.py:43
  135.9 4.4 %copy.28 = bf16[3456,512]{1,0:T(8,128)(2,1)S(1)} copy(bf16[3456,512]{0,1:T(8,128)(2,1)} %bitcast.271) | data formatting | bytes 7077888 | tf_op jit(solution)/shard_map/while/body/eval_jaxpr/vk,vc->kc/dot_general | solution.py:98
  140.3 4.0 %select_add_fusion.2 = f32[27,128,128]{2,1,0:T(8,128)} fusion(f32[27,128,128]{2,1,0:T(8,128)} %get-tuple-element.632, bf16[27,128,512]{2,1,0:T(8,128)(2,1)S(1)} %bitcast.270, pred[]{:T(512)S(6)} %compare.85, bf16[8,512,128]{2,1,0:T(8,128)(2,1)} %get-tuple-element.659, s32[]{:T(128)S(6)} %select_n.170), kind=kOutput, calls=%fused_computation.59.clone.1 | convolution fusion | flops 453869568 | bytes 7208965 | tf_op jit(solution)/shard_map/while/body/eval_jaxpr/vk,vc->kc/dot_general | solution.py:98
  150.1 6.8 %constant_dynamic-slice_fusion.57 = (bf16[8,8,8,128]{3,2,1,0:T(8,128)(2,1)S(1)}, bf16[8,8,8,128]{3,2,1,0:T(8,128)(2,1)S(1)}, bf16[8,8,8,128]{3,2,1,0:T(8,128)(2,...) fusion(bf16[34,18,18,128]{3,2,1,0:T(8,128)(2,1)} %get-tuple-ele, ...), kind=kLoop, calls=%fused_computation.121.clone.1 | loop fusion | bytes 7077924 | tf_op jit(solution)/shard_map/while/body/eval_jaxpr/slice | solution.py:43
  158.1 1.8 copy-done
  159.8 4.4 %copy.28 = bf16[3456,512]{1,0:T(8,128)(2,1)S(1)} copy(bf16[3456,512]{0,1:T(8,128)(2,1)} %bitcast.271) | data formatting | bytes 7077888 | tf_op jit(solution)/shard_map/while/body/eval_jaxpr/vk,vc->kc/dot_general | solution.py:98
  164.3 4.0 %select_add_fusion.2 = f32[27,128,128]{2,1,0:T(8,128)} fusion(f32[27,128,128]{2,1,0:T(8,128)} %get-tuple-element.632, bf16[27,128,512]{2,1,0:T(8,128)(2,1)S(1)} %bitcast.270, pred[]{:T(512)S(6)} %compare.85, bf16[8,512,128]{2,1,0:T(8,128)(2,1)} %get-tuple-element.659, s32[]{:T(128)S(6)} %select_n.170), kind=kOutput, calls=%fused_computation.59.clone.1 | convolution fusion | flops 453869568 | bytes 7208965 | tf_op jit(solution)/shard_map/while/body/eval_jaxpr/vk,vc->kc/dot_general | solution.py:98
  174.1 6.8 %constant_dynamic-slice_fusion.57 = (bf16[8,8,8,128]{3,2,1,0:T(8,128)(2,1)S(1)}, bf16[8,8,8,128]{3,2,1,0:T(8,128)(2,1)S(1)}, bf16[8,8,8,128]{3,2,1,0:T(8,128)(2,...) fusion(bf16[34,18,18,128]{3,2,1,0:T(8,128)(2,1)} %get-tuple-ele, ...), kind=kLoop, calls=%fused_computation.121.clone.1 | loop fusion | bytes 7077924 | tf_op jit(solution)/shard_map/while/body/eval_jaxpr/slice | solution.py:43
  182.0 1.8 copy-done
  183.8 4.4 %copy.28 = bf16[3456,512]{1,0:T(8,128)(2,1)S(1)} copy(bf16[3456,512]{0,1:T(8,128)(2,1)} %bitcast.271) | data formatting | bytes 7077888 | tf_op jit(solution)/shard_map/while/body/eval_jaxpr/vk,vc->kc/dot_general | solution.py:98
  188.2 4.0 %select_add_fusion.2 = f32[27,128,128]{2,1,0:T(8,128)} fusion(f32[27,128,128]{2,1,0:T(8,128)} %get-tuple-element.632, bf16[27,128,512]{2,1,0:T(8,128)(2,1)S(1)} %bitcast.270, pred[]{:T(512)S(6)} %compare.85, bf16[8,512,128]{2,1,0:T(8,128)(2,1)} %get-tuple-element.659, s32[]{:T(128)S(6)} %select_n.170), kind=kOutput, calls=%fused_computation.59.clone.1 | convolution fusion | flops 453869568 | bytes 7208965 | tf_op jit(solution)/shard_map/while/body/eval_jaxpr/vk,vc->kc/dot_general | solution.py:98
  198.1 6.8 %constant_dynamic-slice_fusion.57 = (bf16[8,8,8,128]{3,2,1,0:T(8,128)(2,1)S(1)}, bf16[8,8,8,128]{3,2,1,0:T(8,128)(2,1)S(1)}, bf16[8,8,8,128]{3,2,1,0:T(8,128)(2,...) fusion(bf16[34,18,18,128]{3,2,1,0:T(8,128)(2,1)} %get-tuple-ele, ...), kind=kLoop, calls=%fused_computation.121.clone.1 | loop fusion | bytes 7077924 | tf_op jit(solution)/shard_map/while/body/eval_jaxpr/slice | solution.py:43
  207.8 4.4 %copy.28 = bf16[3456,512]{1,0:T(8,128)(2,1)S(1)} copy(bf16[3456,512]{0,1:T(8,128)(2,1)} %bitcast.271) | data formatting | bytes 7077888 | tf_op jit(solution)/shard_map/while/body/eval_jaxpr/vk,vc->kc/dot_general | solution.py:98
  212.2 4.0 %select_add_fusion.2 = f32[27,128,128]{2,1,0:T(8,128)} fusion(f32[27,128,128]{2,1,0:T(8,128)} %get-tuple-element.632, bf16[27,128,512]{2,1,0:T(8,128)(2,1)S(1)} %bitcast.270, pred[]{:T(512)S(6)} %compare.85, bf16[8,512,128]{2,1,0:T(8,128)(2,1)} %get-tuple-element.659, s32[]{:T(128)S(6)} %select_n.170), kind=kOutput, calls=%fused_computation.59.clone.1 | convolution fusion | flops 453869568 | bytes 7208965 | tf_op jit(solution)/shard_map/while/body/eval_jaxpr/vk,vc->kc/dot_general | solution.py:98
  222.0 6.8 %constant_dynamic-slice_fusion.57 = (bf16[8,8,8,128]{3,2,1,0:T(8,128)(2,1)S(1)}, bf16[8,8,8,128]{3,2,1,0:T(8,128)(2,1)S(1)}, bf16[8,8,8,128]{3,2,1,0:T(8,128)(2,...) fusion(bf16[34,18,18,128]{3,2,1,0:T(8,128)(2,1)} %get-tuple-ele, ...), kind=kLoop, calls=%fused_computation.121.clone.1 | loop fusion | bytes 7077924 | tf_op jit(solution)/shard_map/while/body/eval_jaxpr/slice | solution.py:43
  231.8 4.4 %copy.28 = bf16[3456,512]{1,0:T(8,128)(2,1)S(1)} copy(bf16[3456,512]{0,1:T(8,128)(2,1)} %bitcast.271) | data formatting | bytes 7077888 | tf_op jit(solution)/shard_map/while/body/eval_jaxpr/vk,vc->kc/dot_general | solution.py:98
  236.2 4.0 %select_add_fusion.2 = f32[27,128,128]{2,1,0:T(8,128)} fusion(f32[27,128,128]{2,1,0:T(8,128)} %get-tuple-element.632, bf16[27,128,512]{2,1,0:T(8,128)(2,1)S(1)} %bitcast.270, pred[]{:T(512)S(6)} %compare.85, bf16[8,512,128]{2,1,0:T(8,128)(2,1)} %get-tuple-element.659, s32[]{:T(128)S(6)} %select_n.170), kind=kOutput, calls=%fused_computation.59.clone.1 | convolution fusion | flops 453869568 | bytes 7208965 | tf_op jit(solution)/shard_map/while/body/eval_jaxpr/vk,vc->kc/dot_general | solution.py:98
  242.0 6.1 %select_maximum_fusion = bf16[34,18,18,128]{3,2,1,0:T(8,128)(2,1)} fusion(bf16[34,1,16,128]{3,2,1,0:T(8,128)(2,1)} %collective-permute-done.7, bf16[34,1,16,128]{3,2,1,0:T(8,128)(2,1)} %collective-permute-done.6, bf16[1,16,16,128]{3,2,1,0:T(8,128)(2,1)} %copy-done.10, bf16[32,16,16,128]{3,2,1,0:T(8,128)(2,1)} %bitcast.274, ...), kind=kLoop, calls=%fused_computation.127 | loop fusion | flops 25380864 | bytes 5326848 | tf_op jit(solution)/shard_map/concatenate | solution.py:23
  248.3 105.1 %while.29 = (s32[]{:T(128)}, bf16[8,512,128]{2,1,0:T(8,128)(2,1)S(1)}, s32[8]{0:T(128)S(1)}, s32[8]{0:T(128)S(1)}, bf16[34,18,18,128]{3,2,1,0:T(8,128)(2,1)}, /*...) while((s32[]{:T(128)}, ...), condition=%wide.region_3.4_spmd, body=%wide.region_2.3_spmd.sunk | while | flops 453116480 | bytes 18715932 | solution.py:118
  252.1 7.2 %constant_dynamic-slice_fusion.56 = (bf16[8,8,8,128]{3,2,1,0:T(8,128)(2,1)S(1)}, bf16[8,8,8,128]{3,2,1,0:T(8,128)(2,1)S(1)}, bf16[8,8,8,128]{3,2,1,0:T(8,128)(2,...) fusion(bf16[34,18,18,128]{3,2,1,0:T(8,128)(2,1)} %get-tuple-ele, ...), kind=kLoop, calls=%fused_computation.58.clone.1 | loop fusion | bytes 7077924 | tf_op jit(solution)/shard_map/while/body/eval_jaxpr/slice | solution.py:43
  265.4 8.1 %constant_dynamic-slice_fusion.56 = (bf16[8,8,8,128]{3,2,1,0:T(8,128)(2,1)S(1)}, bf16[8,8,8,128]{3,2,1,0:T(8,128)(2,1)S(1)}, bf16[8,8,8,128]{3,2,1,0:T(8,128)(2,...) fusion(bf16[34,18,18,128]{3,2,1,0:T(8,128)(2,1)} %get-tuple-ele, ...), kind=kLoop, calls=%fused_computation.58.clone.1 | loop fusion | bytes 7077924 | tf_op jit(solution)/shard_map/while/body/eval_jaxpr/slice | solution.py:43
  279.6 7.0 %constant_dynamic-slice_fusion.56 = (bf16[8,8,8,128]{3,2,1,0:T(8,128)(2,1)S(1)}, bf16[8,8,8,128]{3,2,1,0:T(8,128)(2,1)S(1)}, bf16[8,8,8,128]{3,2,1,0:T(8,128)(2,...) fusion(bf16[34,18,18,128]{3,2,1,0:T(8,128)(2,1)} %get-tuple-ele, ...), kind=kLoop, calls=%fused_computation.58.clone.1 | loop fusion | bytes 7077924 | tf_op jit(solution)/shard_map/while/body/eval_jaxpr/slice | solution.py:43
  292.7 6.7 %constant_dynamic-slice_fusion.56 = (bf16[8,8,8,128]{3,2,1,0:T(8,128)(2,1)S(1)}, bf16[8,8,8,128]{3,2,1,0:T(8,128)(2,1)S(1)}, bf16[8,8,8,128]{3,2,1,0:T(8,128)(2,...) fusion(bf16[34,18,18,128]{3,2,1,0:T(8,128)(2,1)} %get-tuple-ele, ...), kind=kLoop, calls=%fused_computation.58.clone.1 | loop fusion | bytes 7077924 | tf_op jit(solution)/shard_map/while/body/eval_jaxpr/slice | solution.py:43
  305.5 6.8 %constant_dynamic-slice_fusion.56 = (bf16[8,8,8,128]{3,2,1,0:T(8,128)(2,1)S(1)}, bf16[8,8,8,128]{3,2,1,0:T(8,128)(2,1)S(1)}, bf16[8,8,8,128]{3,2,1,0:T(8,128)(2,...) fusion(bf16[34,18,18,128]{3,2,1,0:T(8,128)(2,1)} %get-tuple-ele, ...), kind=kLoop, calls=%fused_computation.58.clone.1 | loop fusion | bytes 7077924 | tf_op jit(solution)/shard_map/while/body/eval_jaxpr/slice | solution.py:43
  318.4 6.8 %constant_dynamic-slice_fusion.56 = (bf16[8,8,8,128]{3,2,1,0:T(8,128)(2,1)S(1)}, bf16[8,8,8,128]{3,2,1,0:T(8,128)(2,1)S(1)}, bf16[8,8,8,128]{3,2,1,0:T(8,128)(2,...) fusion(bf16[34,18,18,128]{3,2,1,0:T(8,128)(2,1)} %get-tuple-ele, ...), kind=kLoop, calls=%fused_computation.58.clone.1 | loop fusion | bytes 7077924 | tf_op jit(solution)/shard_map/while/body/eval_jaxpr/slice | solution.py:43
  331.3 6.8 %constant_dynamic-slice_fusion.56 = (bf16[8,8,8,128]{3,2,1,0:T(8,128)(2,1)S(1)}, bf16[8,8,8,128]{3,2,1,0:T(8,128)(2,1)S(1)}, bf16[8,8,8,128]{3,2,1,0:T(8,128)(2,...) fusion(bf16[34,18,18,128]{3,2,1,0:T(8,128)(2,1)} %get-tuple-ele, ...), kind=kLoop, calls=%fused_computation.58.clone.1 | loop fusion | bytes 7077924 | tf_op jit(solution)/shard_map/while/body/eval_jaxpr/slice | solution.py:43
  344.2 6.8 %constant_dynamic-slice_fusion.56 = (bf16[8,8,8,128]{3,2,1,0:T(8,128)(2,1)S(1)}, bf16[8,8,8,128]{3,2,1,0:T(8,128)(2,1)S(1)}, bf16[8,8,8,128]{3,2,1,0:T(8,128)(2,...) fusion(bf16[34,18,18,128]{3,2,1,0:T(8,128)(2,1)} %get-tuple-ele, ...), kind=kLoop, calls=%fused_computation.58.clone.1 | loop fusion | bytes 7077924 | tf_op jit(solution)/shard_map/while/body/eval_jaxpr/slice | solution.py:43
  353.3 25.3 %all-reduce.4.cloned.1.call-done = f32[27,128,128]{2,1,0:T(8,128)} async-done(((f32[27,128,128]{2,1,0:T(8,128)}), f32[27,128,128]{2,1,0:T(8,128)}) %all-reduce.4.cloned.1.call-update) | async-done | bytes 1769488 | tf_op jit(solution)/shard_map/psum | solution.py:109
  378.6 2.9 broadcast_multiply_fusion
  (592 shorter events, 77.5 us)
Async XLA Ops:
  7.2 4.3 %copy-start.12 = (s32[8]{0:T(128)S(1)}, s32[8]{0:T(128)}, u32[]{:S(2)}) copy-start(s32[8]{0:T(128)} %param.13) | copy-start | bytes 100
  7.2 371.5 %all-reduce.4.cloned.1.call-start = ((), (), s32[]{:S(2)}) async-start(), calls=%async_computation | async-start | bytes 3538944 | tf_op jit(solution)/shard_map/psum | solution.py:109
  11.5 8.4 %copy-start.5 = (bf16[8,512,128]{2,1,0:T(8,128)(2,1)}, bf16[8,512,128]{2,1,0:T(8,128)(2,1)S(1)}, u32[]{:S(2)}) copy-start(bf16[8,512,128]{2,1,0:T(8,128)(2,1)S(1)} %get-tuple-element.615) | copy-start | bytes 3145732
  13.1 15.9 %copy-start.3 = (bf16[4,2,2,8,8,8,128]{6,5,2,4,1,3,0:T(8,128)(2,1)}, bf16[4,2,2,8,8,8,128]{6,5,2,4,1,3,0:T(8,128)(2,1)S(1)}, u32[]{:S(2)}) copy-start(bf16[4,2,2,8,8,8,128]{6,5,2,4,1,3,0:T(8,128)(2,1)S(1)} %copy.12) | copy-start | bytes 6291460
  13.1 15.9 %collective-permute-start.1 = (bf16[1,16,16,128]{3,2,1,0:T(8,128)(2,1)S(1)}, bf16[1,16,16,128]{3,2,1,0:T(8,128)(2,1)S(1)}, u32[]{:S(2)}, u32[]{:S(2)}) collective-permute-start(bf16[1,16,16,128]{3,2,1,0:T(8,128)(2,1)S(1)} %get-tuple-element.400), channel_id=1, source_target_pairs={{4,0},{8,4},{12,8},{16,12},{20,16},{24,20},{28,24},{5,1},{9,5},{13... | collective-permute-start | bytes 196616 | tf_op jit(solution)/shard_map/ppermute | solution.py:22
  14.4 14.6 %collective-permute-start = (bf16[1,16,16,128]{3,2,1,0:T(8,128)(2,1)S(1)}, bf16[1,16,16,128]{3,2,1,0:T(8,128)(2,1)S(1)}, u32[]{:S(2)}, u32[]{:S(2)}) collective-permute-start(bf16[1,16,16,128]{3,2,1,0:T(8,128)(2,1)S(1)} %get-tuple-element.399), channel_id=1, source_target_pairs={{0,4},{4,8},{8,12},{12,16},{16,20},{20,24},{24,28},{1,5},{5,9},{9,... | collective-permute-start | bytes 196616 | tf_op jit(solution)/shard_map/ppermute | solution.py:21
  21.1 13.6 %copy-start.7 = (bf16[27,128,128]{2,1,0:T(8,128)(2,1)S(1)}, bf16[27,128,128]{2,1,0:T(8,128)(2,1)}, u32[]{:S(2)}) copy-start(bf16[27,128,128]{2,1,0:T(8,128)(2,1)} %param.10) | copy-start | bytes 2654212
  21.5 15.7 %copy-start.2 = (bf16[4,8,2,8,2,8,128]{6,5,4,3,2,1,0:T(8,128)(2,1)}, bf16[4,8,2,8,2,8,128]{6,5,4,3,2,1,0:T(8,128)(2,1)S(1)}, u32[]{:S(2)}) copy-start(bf16[4,8,2,8,2,8,128]{6,5,4,3,2,1,0:T(8,128)(2,1)S(1)} %copy.13) | copy-start | bytes 6291460
  22.2 14.2 %collective-permute-start.5 = (bf16[1,16,16,128]{3,2,1,0:T(8,128)(2,1)}, bf16[1,16,16,128]{3,2,1,0:T(8,128)(2,1)S(1)}, u32[]{:S(2)}, u32[]{:S(2)}) collective-permute-start(bf16[1,16,16,128]{3,2,1,0:T(8,128)(2,1)} %get-tuple-element.398), channel_id=1, source_target_pairs={{4,0},{8,4},{12,8},{16,12},{20,16},{24,20},{28,24},{5,1},{9,5},{13... | collective-permute-start | bytes 196616 | tf_op jit(solution)/shard_map/ppermute | solution.py:22
  23.5 12.9 %collective-permute-start.4 = (bf16[1,16,16,128]{3,2,1,0:T(8,128)(2,1)}, bf16[1,16,16,128]{3,2,1,0:T(8,128)(2,1)S(1)}, u32[]{:S(2)}, u32[]{:S(2)}) collective-permute-start(bf16[1,16,16,128]{3,2,1,0:T(8,128)(2,1)} %get-tuple-element.397), channel_id=1, source_target_pairs={{0,4},{4,8},{8,12},{12,16},{16,20},{20,24},{24,28},{1,5},{5,9},{9,... | collective-permute-start | bytes 196616 | tf_op jit(solution)/shard_map/ppermute | solution.py:21
  29.7 12.6 %collective-permute-start.3 = (bf16[34,1,16,128]{3,2,1,0:T(8,128)(2,1)}, bf16[34,1,16,128]{3,2,1,0:T(8,128)(2,1)S(1)}, u32[]{:S(2)}, u32[]{:S(2)}) collective-permute-start(bf16[34,1,16,128]{3,2,1,0:T(8,128)(2,1)} %get-tuple-element.396), channel_id=1, source_target_pairs={{1,0},{2,1},{3,2},{5,4},{6,5},{7,6},{9,8},{10,9},{11,10},{13,12},{... | collective-permute-start | bytes 417800 | tf_op jit(solution)/shard_map/ppermute | solution.py:22
  31.0 11.3 %collective-permute-start.2 = (bf16[34,1,16,128]{3,2,1,0:T(8,128)(2,1)S(1)}, bf16[34,1,16,128]{3,2,1,0:T(8,128)(2,1)}, u32[]{:S(2)}, u32[]{:S(2)}) collective-permute-start(bf16[34,1,16,128]{3,2,1,0:T(8,128)(2,1)S(1)} %get-tuple-element.395), channel_id=1, source_target_pairs={{0,1},{1,2},{2,3},{4,5},{5,6},{6,7},{8,9},{9,10},{10,11},{12,13},{... | collective-permute-start | bytes 417800 | tf_op jit(solution)/shard_map/ppermute | solution.py:21
  36.4 5.9 %copy-start.4 = (bf16[4,2,2,8,8,8,128]{6,5,2,4,1,3,0:T(8,128)(2,1)S(1)}, bf16[4,2,2,8,8,8,128]{6,5,2,4,1,3,0:T(8,128)(2,1)}, u32[]{:S(2)}) copy-start(bf16[4,2,2,8,8,8,128]{6,5,2,4,1,3,0:T(8,128)(2,1)} %copy-done.3) | copy-start | bytes 6291460
  36.4 11.5 %copy-start.10 = (bf16[1,16,16,128]{3,2,1,0:T(8,128)(2,1)}, bf16[1,16,16,128]{3,2,1,0:T(8,128)(2,1)S(1)}, u32[]{:S(2)}) copy-start(bf16[1,16,16,128]{3,2,1,0:T(8,128)(2,1)S(1)} %collective-permute-done.5) | copy-start | bytes 196612
  36.4 11.4 %copy-start.11 = (bf16[1,16,16,128]{3,2,1,0:T(8,128)(2,1)}, bf16[1,16,16,128]{3,2,1,0:T(8,128)(2,1)S(1)}, u32[]{:S(2)}) copy-start(bf16[1,16,16,128]{3,2,1,0:T(8,128)(2,1)S(1)} %collective-permute-done.4) | copy-start | bytes 196612
  37.2 204.8 %collective-permute-start.7 = (bf16[34,1,16,128]{3,2,1,0:T(8,128)(2,1)}, bf16[34,1,16,128]{3,2,1,0:T(8,128)(2,1)}, u32[]{:S(2)}, u32[]{:S(2)}) collective-permute-start(bf16[34,1,16,128]{3,2,1,0:T(8,128)(2,1)} %get-tuple-element.394), channel_id=1, source_target_pairs={{1,0},{2,1},{3,2},{5,4},{6,5},{7,6},{9,8},{10,9},{11,10},{13,12},{... | collective-permute-start | bytes 417800 | tf_op jit(solution)/shard_map/ppermute | solution.py:22
  38.6 203.4 %collective-permute-start.6 = (bf16[34,1,16,128]{3,2,1,0:T(8,128)(2,1)}, bf16[34,1,16,128]{3,2,1,0:T(8,128)(2,1)}, u32[]{:S(2)}, u32[]{:S(2)}) collective-permute-start(bf16[34,1,16,128]{3,2,1,0:T(8,128)(2,1)} %get-tuple-element.393), channel_id=1, source_target_pairs={{0,1},{1,2},{2,3},{4,5},{5,6},{6,7},{8,9},{9,10},{10,11},{12,13},{... | collective-permute-start | bytes 417800 | tf_op jit(solution)/shard_map/ppermute | solution.py:21
  61.4 1.8 copy-start
  67.6 3.4 copy-start.1
  67.6 3.4 copy-start.8
  86.1 1.8 copy-start
  92.3 4.0 %copy-start.1 = (bf16[512,3456]{1,0:T(8,128)(2,1)S(1)}, bf16[512,3456]{1,0:T(8,128)(2,1)}, u32[]{:S(2)}) copy-start(bf16[512,3456]{1,0:T(8,128)(2,1)} %copy-done) | copy-start | bytes 10616836 | tf_op jit(solution)/shard_map/while
  92.3 4.0 %copy-start.8 = (bf16[3456,128]{1,0:T(8,128)(2,1)S(1)}, bf16[3456,128]{1,0:T(8,128)(2,1)}, u32[]{:S(2)}) copy-start(bf16[3456,128]{1,0:T(8,128)(2,1)} %get-tuple-element.660) | copy-start | bytes 2654212 | tf_op jit(solution)/shard_map/while
  110.2 1.8 copy-start
  116.4 4.0 %copy-start.1 = (bf16[512,3456]{1,0:T(8,128)(2,1)S(1)}, bf16[512,3456]{1,0:T(8,128)(2,1)}, u32[]{:S(2)}) copy-start(bf16[512,3456]{1,0:T(8,128)(2,1)} %copy-done) | copy-start | bytes 10616836 | tf_op jit(solution)/shard_map/while
  116.4 4.0 %copy-start.8 = (bf16[3456,128]{1,0:T(8,128)(2,1)S(1)}, bf16[3456,128]{1,0:T(8,128)(2,1)}, u32[]{:S(2)}) copy-start(bf16[3456,128]{1,0:T(8,128)(2,1)} %get-tuple-element.660) | copy-start | bytes 2654212 | tf_op jit(solution)/shard_map/while
  134.1 1.8 copy-start
  140.2 4.0 %copy-start.1 = (bf16[512,3456]{1,0:T(8,128)(2,1)S(1)}, bf16[512,3456]{1,0:T(8,128)(2,1)}, u32[]{:S(2)}) copy-start(bf16[512,3456]{1,0:T(8,128)(2,1)} %copy-done) | copy-start | bytes 10616836 | tf_op jit(solution)/shard_map/while
  140.3 4.0 %copy-start.8 = (bf16[3456,128]{1,0:T(8,128)(2,1)S(1)}, bf16[3456,128]{1,0:T(8,128)(2,1)}, u32[]{:S(2)}) copy-start(bf16[3456,128]{1,0:T(8,128)(2,1)} %get-tuple-element.660) | copy-start | bytes 2654212 | tf_op jit(solution)/shard_map/while
  158.0 1.8 copy-start
  164.2 4.0 %copy-start.1 = (bf16[512,3456]{1,0:T(8,128)(2,1)S(1)}, bf16[512,3456]{1,0:T(8,128)(2,1)}, u32[]{:S(2)}) copy-start(bf16[512,3456]{1,0:T(8,128)(2,1)} %copy-done) | copy-start | bytes 10616836 | tf_op jit(solution)/shard_map/while
  164.2 4.0 %copy-start.8 = (bf16[3456,128]{1,0:T(8,128)(2,1)S(1)}, bf16[3456,128]{1,0:T(8,128)(2,1)}, u32[]{:S(2)}) copy-start(bf16[3456,128]{1,0:T(8,128)(2,1)} %get-tuple-element.660) | copy-start | bytes 2654212 | tf_op jit(solution)/shard_map/while
  182.0 1.8 copy-start
  188.2 4.0 %copy-start.1 = (bf16[512,3456]{1,0:T(8,128)(2,1)S(1)}, bf16[512,3456]{1,0:T(8,128)(2,1)}, u32[]{:S(2)}) copy-start(bf16[512,3456]{1,0:T(8,128)(2,1)} %copy-done) | copy-start | bytes 10616836 | tf_op jit(solution)/shard_map/while
  188.2 4.0 %copy-start.8 = (bf16[3456,128]{1,0:T(8,128)(2,1)S(1)}, bf16[3456,128]{1,0:T(8,128)(2,1)}, u32[]{:S(2)}) copy-start(bf16[3456,128]{1,0:T(8,128)(2,1)} %get-tuple-element.660) | copy-start | bytes 2654212 | tf_op jit(solution)/shard_map/while
  206.0 1.8 copy-start
  212.2 4.0 %copy-start.1 = (bf16[512,3456]{1,0:T(8,128)(2,1)S(1)}, bf16[512,3456]{1,0:T(8,128)(2,1)}, u32[]{:S(2)}) copy-start(bf16[512,3456]{1,0:T(8,128)(2,1)} %copy-done) | copy-start | bytes 10616836 | tf_op jit(solution)/shard_map/while
  212.2 4.0 %copy-start.8 = (bf16[3456,128]{1,0:T(8,128)(2,1)S(1)}, bf16[3456,128]{1,0:T(8,128)(2,1)}, u32[]{:S(2)}) copy-start(bf16[3456,128]{1,0:T(8,128)(2,1)} %get-tuple-element.660) | copy-start | bytes 2654212 | tf_op jit(solution)/shard_map/while
  230.0 1.8 copy-start
  236.2 4.0 %copy-start.1 = (bf16[512,3456]{1,0:T(8,128)(2,1)S(1)}, bf16[512,3456]{1,0:T(8,128)(2,1)}, u32[]{:S(2)}) copy-start(bf16[512,3456]{1,0:T(8,128)(2,1)} %copy-done) | copy-start | bytes 10616836 | tf_op jit(solution)/shard_map/while
  236.2 4.0 %copy-start.8 = (bf16[3456,128]{1,0:T(8,128)(2,1)S(1)}, bf16[3456,128]{1,0:T(8,128)(2,1)}, u32[]{:S(2)}) copy-start(bf16[3456,128]{1,0:T(8,128)(2,1)} %get-tuple-element.660) | copy-start | bytes 2654212 | tf_op jit(solution)/shard_map/while
  242.0 6.3 %copy-start.9 = (bf16[27,128,128]{2,1,0:T(8,128)(2,1)S(1)}, bf16[27,128,128]{2,1,0:T(8,128)(2,1)}, u32[]{:S(2)}) copy-start(bf16[27,128,128]{2,1,0:T(8,128)(2,1)} %copy.14) | copy-start | bytes 2654212
  353.3 28.2 %copy-start.6 = (bf16[8,512,128]{2,1,0:T(8,128)(2,1)}, bf16[8,512,128]{2,1,0:T(8,128)(2,1)S(1)}, u32[]{:S(2)}) copy-start(bf16[8,512,128]{2,1,0:T(8,128)(2,1)S(1)} %get-tuple-element.272) | copy-start | bytes 3145732
Sparse Core Ops, SparseCore 0:
  242.1 136.4 all-reduce.3
where the time goes:
time: 391 us; the launch traced here: 388 us
  local copies, waits for them, and re-layouts  202 us (52%)
  matrix products  55.7 us (14%)
  loops' own time  47.4 us (12%)
  waiting for transfers between devices  25.3 us (6%)
  starting transfers between devices  23.6 us (6%)
  other arithmetic  20.4 us (5%)
  between operations  14.3 us (4%)
    slice x16, local copies, waits for them, and re-layouts, brick_patches(): block[along_x + 1:along_x + 1 + BRICK, along_y + 1:along_y + 1 + BRICK, a...  113 us
    dot_general x8, local copies, waits for them, and re-layouts, forward_step(): jnp.einsum('vk,vc->kc', patches, masked_cot[slot_index], preferred_elemen...  35 us
    dot_general x8, matrix products, forward_step(): jnp.einsum('vk,vc->kc', patches, masked_cot[slot_index], preferred_elemen...  31.3 us
    while x464, local copies, waits for them, and re-layouts  28.1 us
    psum x1, waiting for transfers between devices, shards(): grad_weight = lax.psum(local_grad, ('gx', 'gy')) * scale  25.3 us
    another operation x1, loops' own time, shards(): lax.scan(make_forward(), jnp.zeros((27, channels, channels), jnp.float32)...  24.3 us
    another operation x1, loops' own time, shards(): lax.scan(backward_step, jnp.zeros((), jnp.float32), slot_ids)  23.1 us
    ppermute x4, starting transfers between devices, with_halo(): before = lax.ppermute(last, axis, up)  18.3 us
  transfers between devices with their start and end apart: 9, of which 1 were waited for; matrix products, arithmetic and copies ran while one was open for 66% of the time, Pallas kernels for 0%

commit v1 on v0

v1 whole, which is shorter than its diff:
```python
import functools
import math

import jax
import jax.numpy as jnp
from jax import lax
from jax.experimental import pallas as pl
from jax.experimental.pallas import tpu as pltpu
from jax.sharding import PartitionSpec as P

BRICK = 8
REGION_X = 4
REGION_Y = 2
REGION_Z = 2
FACE = BRICK * BRICK
VMEM_LIMIT = 56 * 1024 * 1024
BF16 = jnp.bfloat16
F32 = jnp.float32


def over_rows(a, b):
    return lax.dot_general(a, b, (((0,), (0,)), ((), ())), preferred_element_type=F32)


def slot_mask(occ_ref, slot):
    slots = occ_ref.shape[0]
    chosen = lax.broadcasted_iota(jnp.int32, (slots, 128), 0) == slot
    on = occ_ref[...].astype(F32)
    return over_rows(on, chosen.astype(F32))


def place_kernel(pos_ref, occ_ref, feat_ref, cot_ref, gx_ref, gd_ref, mc_ref):
    for grid in (gx_ref, gd_ref):
        grid[...] = jnp.zeros_like(grid)

    @pl.loop(0, feat_ref.shape[0])
    def _(slot):
        at = pos_ref[slot]
        keep = slot_mask(occ_ref, slot) * (at >= 0).astype(F32)
        mc = jnp.where(keep > 0.5, cot_ref[slot].astype(F32), 0.0).astype(BF16)
        mx = jnp.where(keep > 0.5, feat_ref[slot].astype(F32), 0.0).astype(BF16)
        mc_ref[slot] = mc

        @pl.when(at >= 0)
        def _():
            bx = at // (REGION_Y * REGION_Z)
            by = at // REGION_Z % REGION_Y
            bz = at % REGION_Z
            rows = pl.ds(pl.multiple_of(by * FACE, FACE), FACE)
            for a in range(BRICK):
                gx_ref[bz, bx * BRICK + a, rows, :] = mx[a * FACE : (a + 1) * FACE]
                gd_ref[bz, bx * BRICK + a, rows, :] = mc[a * FACE : (a + 1) * FACE]


def expand(at, wide, patches):
    at = jnp.maximum(at, 0)
    bx = at // (REGION_Y * REGION_Z)
    by = at // REGION_Z % REGION_Y
    bz = at % REGION_Z
    rows = pl.ds(pl.multiple_of(by * FACE, FACE), FACE + 2 * BRICK)
    spot = lax.broadcasted_iota(jnp.int32, (BRICK + 2, BRICK, 128), 1)
    upper = (bz == 1).astype(F32)
    for x in range(BRICK + 2):
        this = wide[bz, bx * BRICK + x, rows, :].reshape(BRICK + 2, BRICK, 128)
        other = wide[1 - bz, bx * BRICK + x, rows, :].reshape(BRICK + 2, BRICK, 128)
        below = jnp.where(
            spot == 0, pltpu.roll(other, 1, 1) * upper, pltpu.roll(this, 1, 1)
        )
        above = jnp.where(
            spot == BRICK - 1,
            pltpu.roll(other, BRICK - 1, 1) * (1.0 - upper),
            pltpu.roll(this, BRICK - 1, 1),
        )
        for r, moved in enumerate((below, this, above)):
            for q in range(3):
                lanes = slice((q * 3 + r) * 128, (q * 3 + r + 1) * 128)
                patches[x * FACE : (x + 1) * FACE, lanes] = (
                    moved[q : q + BRICK].reshape(FACE, 128).astype(BF16)
                )


def widen(grid, wide):
    @pl.loop(0, grid.shape[1])
    def _(x):
        for bz in range(REGION_Z):
            wide[bz, x] = grid[bz, x].astype(F32)


def wgrad_kernel(scale, pos_ref, gx_ref, mc_ref, out_ref, wide, patches):
    widen(gx_ref, wide)
    out_ref[...] = jnp.zeros_like(out_ref)

    @pl.loop(0, mc_ref.shape[0])
    def _(slot):
        expand(pos_ref[slot], wide, patches)
        for p in range(3):
            part = patches[p * FACE : p * FACE + BRICK * FACE]
            out_ref[p] += over_rows(mc_ref[slot], part) * scale


def conv_kernel(pos_ref, occ_ref, gx_ref, gd_ref, wf_ref, wb_ref, out_ref, gi_ref, wide, patches):
    for grid, weight, result in ((gx_ref, wf_ref, out_ref), (gd_ref, wb_ref, gi_ref)):
        widen(grid, wide)

        @pl.loop(0, result.shape[0])
        def _(slot):
            at = pos_ref[slot]
            expand(at, wide, patches)
            keep = slot_mask(occ_ref, slot) * (at >= 0).astype(F32)
            total = jnp.zeros((BRICK * FACE, 128), F32)
            for p in range(3):
                part = patches[p * FACE : p * FACE + BRICK * FACE]
                total += jnp.dot(part, weight[p], preferred_element_type=F32)
            result[slot] = jnp.where(keep > 0.5, total, 0.0).astype(BF16)


def with_halo(value, sides):
    for axis, dim, width in sides:
        size, length = (lax.axis_size(axis), value.shape[dim])
        up = [(i, (i + 1) % size) for i in range(size - 1)]
        down = [(j, i) for i, j in up]
        last = lax.slice_in_dim(value, length - width, length, axis=dim)
        leading = lax.slice_in_dim(value, 0, width, axis=dim)
        before = lax.ppermute(last, axis, up)
        after = lax.ppermute(leading, axis, down)
        value = jnp.concatenate([before, value, after], axis=dim)
    return value


def shards(features, weights, cotangent, occupancy, slot_pos):
    slots, voxels, channels = features.shape
    devices = lax.axis_size("gx") * lax.axis_size("gy")
    scale = 1.0 / math.sqrt(float(devices * slots * voxels))
    vmem = pl.BlockSpec(memory_space=pltpu.VMEM)
    smem = pl.BlockSpec(memory_space=pltpu.SMEM)
    params = pltpu.CompilerParams(vmem_limit_bytes=VMEM_LIMIT)
    grid_shape = (REGION_Z, REGION_X * BRICK, REGION_Y * FACE, channels)
    wide_shape = (REGION_Z, REGION_X * BRICK + 2, REGION_Y * FACE + 2 * BRICK, channels)
    scratch = [
        pltpu.VMEM(wide_shape, F32),
        pltpu.VMEM(((BRICK + 2) * FACE, 9 * channels), BF16),
    ]
    bricks = jax.ShapeDtypeStruct(features.shape, BF16)

    gx, gd, mc = pl.pallas_call(
        place_kernel,
        out_shape=[jax.ShapeDtypeStruct(grid_shape, BF16)] * 2 + [bricks],
        in_specs=[smem, vmem, vmem, vmem],
        out_specs=[vmem] * 3,
        compiler_params=params,
        name="place",
    )(slot_pos, occupancy, features, cotangent)

    sides = (("gx", 1, 1), ("gy", 2, BRICK))
    gx = with_halo(gx, sides)
    local = pl.pallas_call(
        functools.partial(wgrad_kernel, scale),
        out_shape=jax.ShapeDtypeStruct((3, channels, 9 * channels), F32),
        in_specs=[smem, vmem, vmem],
        out_specs=vmem,
        scratch_shapes=scratch,
        compiler_params=params,
        name="wgrad",
    )(slot_pos, gx, mc)
    summed = lax.psum(local, ("gx", "gy"))
    grad_weight = (
        summed.reshape(3, channels, 9, channels).transpose(0, 2, 3, 1).reshape(27, channels, channels)
    )

    gd = with_halo(gd, sides)
    w_forward = weights.reshape(3, 9 * channels, channels)
    w_backward = weights[::-1].transpose(0, 2, 1).reshape(3, 9 * channels, channels)
    outputs, grad_input = pl.pallas_call(
        conv_kernel,
        out_shape=[bricks, bricks],
        in_specs=[smem] + [vmem] * 5,
        out_specs=[vmem, vmem],
        scratch_shapes=scratch,
        compiler_params=params,
        cost_estimate=pl.CostEstimate(
            flops=4 * slots * voxels * 27 * channels * channels, bytes_accessed=8 << 20, transcendentals=0
        ),
        name="conv",
    )(slot_pos, occupancy, gx, gd, w_forward, w_backward)
    return (outputs, grad_input, grad_weight)


def solution(mesh):
    return jax.shard_map(
        shards,
        mesh=mesh,
        in_specs=(
            P(("gx", "gy"), None, None),
            P(),
            P(("gx", "gy"), None, None),
            P(("gx", "gy"), None),
            P(("gx", "gy")),
        ),
        out_specs=(P(("gx", "gy"), None, None), P(("gx", "gy"), None, None), P()),
        check_vma=False,
    )
```

time: 391 us -> 203 us (0.52)
  local copies, waits for them, and re-layouts: 202 us -> 13.5 us
  waiting for transfers between devices: 25.3 us -> 110 us
  matrix products: 55.7 us -> 0 us
  loops' own time: 47.4 us -> 0 us
  Pallas kernels: 0 us -> 41.5 us
  other arithmetic: 20.4 us -> 3.42 us
    slice x16 -> x2, local copies, waits for them, and re-layouts: 113 us -> 1.77 us  [with_halo(): leading = lax.slice_in_dim(value, 0, width, axis=dim)]
    psum x1, waiting for transfers between devices: 25.3 us -> 109 us  [shards(): summed = lax.psum(local, ('gx', 'gy'))]
    dot_general x26 -> x0, matrix products: 55.7 us -> none  [the longest x8 31.3 us: forward_step(): jnp.einsum('vk,vc->kc', patches, masked_cot[slot_index], preferred_elemen...]
    another operation x2 -> x0, loops' own time: 47.4 us -> none  [the longest x1 24.3 us: shards(): lax.scan(make_forward(), jnp.zeros((27, channels, channels), jnp.float32)...]
    pallas_call x0 -> x3, Pallas kernels: none -> 41.5 us  [the longest x1 24.1 us: shards(): pl.pallas_call(conv_kernel, out_shape=[bricks, bricks], in_specs=[smem] +...]
    dot_general x8 -> x0, local copies, waits for them, and re-layouts: 35 us -> none  [forward_step(): jnp.einsum('vk,vc->kc', patches, masked_cot[slot_index], preferred_elemen...]
    while x464 -> x0, local copies, waits for them, and re-layouts: 28.1 us -> none
    dynamic_slice x32 -> x0, local copies, waits for them, and re-layouts: 19.8 us -> none  [the longest x16 9.91 us: brick_corner(): position = jnp.maximum(slot_pos[slot_index], 0)]
  transfers between devices with their start and end apart: 9 -> 9, of which waited for: 1 -> 2; matrix products, arithmetic and copies ran while one was open for 66% -> 7% of each run, Pallas kernels for 0% -> 17%
where the time goes in v1:
time: 203 us
  waiting for transfers between devices  110 us (54%)
  Pallas kernels  41.5 us (20%)
  starting transfers between devices  20.6 us (10%)
  between operations  14.2 us (7%)
  local copies, waits for them, and re-layouts  13.5 us (7%)
  other arithmetic  3.42 us (2%)
    psum x1, waiting for transfers between devices, shards(): summed = lax.psum(local, ('gx', 'gy'))  109 us
    pallas_call x1, Pallas kernels, shards(): pl.pallas_call(conv_kernel, out_shape=[bricks, bricks], in_specs=[smem] +...  24.1 us
    ppermute x4, starting transfers between devices, with_halo(): before = lax.ppermute(last, axis, up)  15.4 us
    pallas_call x1, Pallas kernels, shards(): pl.pallas_call(functools.partial(wgrad_kernel, scale), out_shape=jax.Shap...  10.6 us
    pallas_call x1, Pallas kernels, shards(): pl.pallas_call(place_kernel, out_shape=[jax.ShapeDtypeStruct(grid_shape,...  6.76 us
    unnamed x7, local copies, waits for them, and re-layouts  5.28 us
    ppermute x4, starting transfers between devices, with_halo(): after = lax.ppermute(leading, axis, down)  5.17 us
  transfers between devices with their start and end apart: 9, of which 2 were waited for; matrix products, arithmetic and copies ran while one was open for 7% of the time, Pallas kernels for 17%

profile of v1, /device:TPU:0, one launch (start us, length us, event | category | flops | bytes accessed | tf_op | source)
XLA Modules:
  0.0 202.7 jit_solution(18431876251979293198)
XLA Ops:
  7.2 0.0 all-reduce.2.cloned.1.call-start
  7.2 6.8 %place.1 = (bf16[2,32,128,128]{3,2,1,0:T(8,128)(2,1)}, bf16[2,32,128,128]{3,2,1,0:T(8,128)(2,1)}, bf16[8,512,128]{2,1,0:T(8,128)(2,1)}) custom-call(s32[8]{0:T(128)} %pos_ref.5, s32[8,512]{1,0:T(8,128)} %occ_ref.3, bf16[8,512,128]{2,1,0:T(8,128)(2,1)} %feat_ref.1, bf16[8,512,128]{2,1,0:T(8,128)(2,1)} %cot_ref.1), custom_call_target="tpu_custom_call" | custom-call | tf_op jit(solution)/shard_map/place/pallas_call | solution.py:145
  14.0 0.9 fusion.3
  14.9 4.8 %collective-permute-start = (bf16[2,1,128,128]{3,2,1,0:T(8,128)(2,1)S(1)}, bf16[2,1,128,128]{3,2,1,0:T(8,128)(2,1)S(1)}, u32[]{:S(2)}, u32[]{:S(2)}) collective-permute-start(bf16[2,1,128,128]{3,2,1,0:T(8,128)(2,1)S(1)} %get-tuple-element.20), channel_id=1, source_target_pairs={{0,4},{4,8},{8,12},{12,16},{16,20},{20,24},{24,28},{1,5},{5,9},{9,... | collective-permute-start | bytes 196616 | tf_op jit(solution)/shard_map/ppermute | solution.py:124
  19.7 1.3 collective-permute-start.1
  21.0 0.9 fusion.2
  21.9 4.5 %collective-permute-start.4 = (bf16[2,1,128,128]{3,2,1,0:T(8,128)(2,1)S(1)}, bf16[2,1,128,128]{3,2,1,0:T(8,128)(2,1)S(1)}, u32[]{:S(2)}, u32[]{:S(2)}) collective-permute-start(bf16[2,1,128,128]{3,2,1,0:T(8,128)(2,1)S(1)} %get-tuple-element.18), channel_id=1, source_target_pairs={{0,4},{4,8},{8,12},{12,16},{16,20},{20,24},{24,28},{1,5},{5,9},{9,... | collective-permute-start | bytes 196616 | tf_op jit(solution)/shard_map/ppermute | solution.py:124
  26.5 1.3 collective-permute-start.5
  27.8 0.0 collective-permute-done
  27.8 0.0 copy-start
  27.8 2.1 %constant_dynamic-update-slice_fusion.1 = bf16[2,34,128,128]{3,2,1,0:T(8,128)(2,1)S(1)} fusion(bf16[2,34,128,128]{3,2,1,0:T(8,128)(2,1)S(1)} %constant_dynamic-update-slice_fusion.2, bf16[2,32,128,128]{3,2,1,0:T(8,128)(2,1)} %get-tuple-element.8), kind=kLoop, calls=%fused_computation.4 | loop fusion | bytes 4194304
  29.9 0.0 collective-permute-done.1
  29.9 0.1 fusion.1
  30.0 1.3 collective-permute-start.2
  31.3 1.3 collective-permute-start.3
  32.6 0.0 collective-permute-done.4
  32.6 0.0 copy-done
  32.6 0.3 constant_dynamic-update-slice_fusion.4
  32.9 0.2 collective-permute-done.5
  33.1 0.7 fusion
  33.8 4.7 %collective-permute-start.6 = (bf16[2,34,8,128]{3,2,1,0:T(8,128)(2,1)}, bf16[2,34,8,128]{3,2,1,0:T(8,128)(2,1)S(1)}, u32[]{:S(2)}, u32[]{:S(2)}) collective-permute-start(bf16[2,34,8,128]{3,2,1,0:T(8,128)(2,1)} %get-tuple-element.13), channel_id=1, source_target_pairs={{0,1},{1,2},{2,3},{4,5},{5,6},{6,7},{8,9},{9,10},{10,11},{12,13},{... | collective-permute-start | bytes 417800 | tf_op jit(solution)/shard_map/ppermute | solution.py:124
  38.5 1.3 collective-permute-start.7
  39.8 0.0 collective-permute-done.2
  39.8 0.0 collective-permute-done.3
  39.9 1.7 pad_maximum_fusion.gx_ref
  41.6 10.6 %wgrad.1 = f32[3,128,1152]{2,1,0:T(8,128)} custom-call(s32[8]{0:T(128)} %pos_ref.5, bf16[2,34,144,128]{3,2,1,0:T(8,128)(2,1)} %pad_maximum_fusion.gx_ref, bf16[8,512,128]{2,1,0:T(8,128)(2,1)} %get-tuple-element.12.mc_ref), custom_call_target="tpu_custom_call" | custom-call | tf_op jit(solution)/shard_map/wgrad/pallas_call | solution.py:156
  52.1 2.8 %copy.11 = f32[3,128,1152]{1,2,0:T(8,128)} copy(f32[3,128,1152]{2,1,0:T(8,128)} %wgrad.1) | data formatting | bytes 3538944 | tf_op jit(solution)/shard_map/wgrad/pallas_call | solution.py:156
  55.0 0.0 all-reduce.2.cloned.1.call-update
  55.0 1.2 reverse_bitcast_fusion
  56.2 1.6 copy.10
  57.9 0.0 collective-permute-done.6
  57.9 0.0 collective-permute-done.7
  57.9 1.7 pad_maximum_fusion.1.gd_ref
  59.6 24.1 %conv.1 = (bf16[8,512,128]{2,1,0:T(8,128)(2,1)}, bf16[8,512,128]{2,1,0:T(8,128)(2,1)}) custom-call(s32[8]{0:T(128)} %pos_ref.5, s32[8,512]{1,0:T(8,128)} %occ_ref.3, bf16[2,34,144,128]{3,2,1,0:T(8,128)(2,1)} %pad_maximum_fusion.gx_ref, bf16[2,34,144,128]{3,2,1,0:T(8,128)(2,1)} %pad_maximum_fusion.1.gd_ref, bf16[3,1152,128]{2,1,0:T(8,128)(2,1)} %bitcast.10, ...), custom_call_target="tpu_custom_call" | custom-call | flops 7247757312 | bytes 8388608 | tf_op jit(solution)/shard_map/conv/pallas_call | solution.py:173
  83.7 109.3 %all-reduce.2.cloned.1.call-done = f32[27,128,128]{2,1,0:T(8,128)} async-done(((f32[27,128,128]{2,1,0:T(8,128)}), f32[27,128,128]{2,1,0:T(8,128)}) %all-reduce.2.cloned.1.call-update) | async-done | bytes 1769488 | tf_op jit(solution)/shard_map/psum | solution.py:165
  193.0 2.9 %copy.17 = f32[27,128,128]{2,1,0:T(8,128)} copy(f32[27,128,128]{2,1,0:T(8,128)} %all-reduce.2.cloned.1.call-done) | data formatting | bytes 3538944
  (4 shorter events, 0.0 us)
Async XLA Ops:
  7.2 185.8 %all-reduce.2.cloned.1.call-start = ((), (), s32[]{:S(2)}) async-start(), calls=%async_computation | async-start | bytes 3538944 | tf_op jit(solution)/shard_map/psum | solution.py:165
  14.9 12.9 %collective-permute-start = (bf16[2,1,128,128]{3,2,1,0:T(8,128)(2,1)S(1)}, bf16[2,1,128,128]{3,2,1,0:T(8,128)(2,1)S(1)}, u32[]{:S(2)}, u32[]{:S(2)}) collective-permute-start(bf16[2,1,128,128]{3,2,1,0:T(8,128)(2,1)S(1)} %get-tuple-element.20), channel_id=1, source_target_pairs={{0,4},{4,8},{8,12},{12,16},{16,20},{20,24},{24,28},{1,5},{5,9},{9,... | collective-permute-start | bytes 196616 | tf_op jit(solution)/shard_map/ppermute | solution.py:124
  19.7 10.2 %collective-permute-start.1 = (bf16[2,1,128,128]{3,2,1,0:T(8,128)(2,1)S(1)}, bf16[2,1,128,128]{3,2,1,0:T(8,128)(2,1)S(1)}, u32[]{:S(2)}, u32[]{:S(2)}) collective-permute-start(bf16[2,1,128,128]{3,2,1,0:T(8,128)(2,1)S(1)} %get-tuple-element.19), channel_id=1, source_target_pairs={{4,0},{8,4},{12,8},{16,12},{20,16},{24,20},{28,24},{5,1},{9,5},{13... | collective-permute-start | bytes 196616 | tf_op jit(solution)/shard_map/ppermute | solution.py:125
  21.9 10.7 %collective-permute-start.4 = (bf16[2,1,128,128]{3,2,1,0:T(8,128)(2,1)S(1)}, bf16[2,1,128,128]{3,2,1,0:T(8,128)(2,1)S(1)}, u32[]{:S(2)}, u32[]{:S(2)}) collective-permute-start(bf16[2,1,128,128]{3,2,1,0:T(8,128)(2,1)S(1)} %get-tuple-element.18), channel_id=1, source_target_pairs={{0,4},{4,8},{8,12},{12,16},{16,20},{20,24},{24,28},{1,5},{5,9},{9,... | collective-permute-start | bytes 196616 | tf_op jit(solution)/shard_map/ppermute | solution.py:124
  26.5 6.7 %collective-permute-start.5 = (bf16[2,1,128,128]{3,2,1,0:T(8,128)(2,1)S(1)}, bf16[2,1,128,128]{3,2,1,0:T(8,128)(2,1)S(1)}, u32[]{:S(2)}, u32[]{:S(2)}) collective-permute-start(bf16[2,1,128,128]{3,2,1,0:T(8,128)(2,1)S(1)} %get-tuple-element.17), channel_id=1, source_target_pairs={{4,0},{8,4},{12,8},{16,12},{20,16},{24,20},{28,24},{5,1},{9,5},{13... | collective-permute-start | bytes 196616 | tf_op jit(solution)/shard_map/ppermute | solution.py:125
  27.8 4.9 %copy-start = (bf16[2,32,128,128]{3,2,1,0:T(8,128)(2,1)S(1)}, bf16[2,32,128,128]{3,2,1,0:T(8,128)(2,1)}, u32[]{:S(2)}) copy-start(bf16[2,32,128,128]{3,2,1,0:T(8,128)(2,1)} %get-tuple-element.9) | copy-start | bytes 6291460
  30.0 9.8 %collective-permute-start.2 = (bf16[2,34,8,128]{3,2,1,0:T(8,128)(2,1)S(1)}, bf16[2,34,8,128]{3,2,1,0:T(8,128)(2,1)S(1)}, u32[]{:S(2)}, u32[]{:S(2)}) collective-permute-start(bf16[2,34,8,128]{3,2,1,0:T(8,128)(2,1)S(1)} %get-tuple-element.15), channel_id=1, source_target_pairs={{0,1},{1,2},{2,3},{4,5},{5,6},{6,7},{8,9},{9,10},{10,11},{12,13},{... | collective-permute-start | bytes 417800 | tf_op jit(solution)/shard_map/ppermute | solution.py:124
  31.3 8.5 %collective-permute-start.3 = (bf16[2,34,8,128]{3,2,1,0:T(8,128)(2,1)S(1)}, bf16[2,34,8,128]{3,2,1,0:T(8,128)(2,1)S(1)}, u32[]{:S(2)}, u32[]{:S(2)}) collective-permute-start(bf16[2,34,8,128]{3,2,1,0:T(8,128)(2,1)S(1)} %get-tuple-element.16), channel_id=1, source_target_pairs={{1,0},{2,1},{3,2},{5,4},{6,5},{7,6},{9,8},{10,9},{11,10},{13,12},{... | collective-permute-start | bytes 417800 | tf_op jit(solution)/shard_map/ppermute | solution.py:125
  33.8 24.0 %collective-permute-start.6 = (bf16[2,34,8,128]{3,2,1,0:T(8,128)(2,1)}, bf16[2,34,8,128]{3,2,1,0:T(8,128)(2,1)S(1)}, u32[]{:S(2)}, u32[]{:S(2)}) collective-permute-start(bf16[2,34,8,128]{3,2,1,0:T(8,128)(2,1)} %get-tuple-element.13), channel_id=1, source_target_pairs={{0,1},{1,2},{2,3},{4,5},{5,6},{6,7},{8,9},{9,10},{10,11},{12,13},{... | collective-permute-start | bytes 417800 | tf_op jit(solution)/shard_map/ppermute | solution.py:124
  38.5 19.3 %collective-permute-start.7 = (bf16[2,34,8,128]{3,2,1,0:T(8,128)(2,1)S(1)}, bf16[2,34,8,128]{3,2,1,0:T(8,128)(2,1)S(1)}, u32[]{:S(2)}, u32[]{:S(2)}) collective-permute-start(bf16[2,34,8,128]{3,2,1,0:T(8,128)(2,1)S(1)} %get-tuple-element.14), channel_id=1, source_target_pairs={{1,0},{2,1},{3,2},{5,4},{6,5},{7,6},{9,8},{10,9},{11,10},{13,12},{... | collective-permute-start | bytes 417800 | tf_op jit(solution)/shard_map/ppermute | solution.py:125
Sparse Core Ops, SparseCore 0:
  55.1 137.8 all-reduce.1

commit v2 on v1

--- a/solution.py
+++ b/solution.py
@@ -127,6 +127,40 @@
     return value
 
 
+def total_over(value, steps):
+    sent = []
+    for axis, stride in steps:
+        size = lax.axis_size(axis)
+        pairs = [(i, i ^ stride) for i in range(size)]
+        bit = (lax.axis_index(axis) // stride) % 2
+        half = value.shape[0] // 2
+        mine = lax.dynamic_slice_in_dim(value, bit * half, half, axis=0)
+        other = lax.dynamic_slice_in_dim(value, (1 - bit) * half, half, axis=0)
+        value = mine + lax.ppermute(other, axis, pairs)
+        sent.append((axis, pairs, bit))
+    for axis, pairs, bit in reversed(sent):
+        other = lax.ppermute(value, axis, pairs)
+        low = jnp.where(bit == 0, value, other)
+        high = jnp.where(bit == 0, other, value)
+        value = jnp.concatenate([low, high], axis=0)
+    return value
+
+
+def axis_steps(axis):
+    return [(axis, 1 << k) for k in range(lax.axis_size(axis).bit_length() - 1)]
+
+
+def all_sum(value):
+    rows = value.shape[0]
+    unit = 2 * 8 * lax.axis_size("gx") * lax.axis_size("gy")
+    padded = -(-rows // unit) * unit
+    value = jnp.pad(value, ((0, padded - rows), (0, 0)))
+    along_x, along_y = axis_steps("gx"), axis_steps("gy")
+    first = total_over(value[: padded // 2], along_y + along_x)
+    second = total_over(value[padded // 2 :], along_y[:1] + along_x + along_y[1:])
+    return jnp.concatenate([first, second], axis=0)[:rows]
+
+
 def shards(features, weights, cotangent, occupancy, slot_pos):
     slots, voxels, channels = features.shape
     devices = lax.axis_size("gx") * lax.axis_size("gy")
@@ -162,10 +196,9 @@
         compiler_params=params,
         name="wgrad",
     )(slot_pos, gx, mc)
-    summed = lax.psum(local, ("gx", "gy"))
-    grad_weight = (
-        summed.reshape(3, channels, 9, channels).transpose(0, 2, 3, 1).reshape(27, channels, channels)
-    )
+    local = local.reshape(3, channels, 9, channels).transpose(0, 2, 3, 1)
+    summed = all_sum(local.reshape(27 * channels, channels))
+    grad_weight = summed.reshape(27, channels, channels)
 
     gd = with_halo(gd, sides)
     w_forward = weights.reshape(3, 9 * channels, channels)

time: 203 us -> 135 us (0.67)
  waiting for transfers between devices: 110 us -> 19.7 us
  starting transfers between devices: 20.6 us -> 51.6 us
  between operations: 14.2 us -> 1.27 us
  other arithmetic: 3.42 us -> 6.94 us
    psum x1 -> x0, waiting for transfers between devices: 109 us -> none  [shards(): summed = lax.psum(local, ('gx', 'gy'))]
    ppermute x0 -> x20, starting transfers between devices: none -> 31 us  [the longest x10 20.2 us: total_over(): value = mine + lax.ppermute(other, axis, pairs)]
    ppermute x0 -> x20, waiting for transfers between devices: none -> 19.7 us  [the longest x10 11.1 us: total_over(): other = lax.ppermute(value, axis, pairs)]
    unnamed x7 -> x12, local copies, waits for them, and re-layouts: 5.28 us -> 5.36 us
  transfers between devices with their start and end apart: 9 -> 28, of which waited for: 2 -> 11; matrix products, arithmetic and copies ran while one was open for 7% -> 10% of each run, Pallas kernels for 17% -> 18%
where the time goes in v2:
time: 135 us; the launch traced here: 134 us
  starting transfers between devices  51.6 us (38%)
  Pallas kernels  41.5 us (31%)
  waiting for transfers between devices  19.7 us (15%)
  local copies, waits for them, and re-layouts  13 us (10%)
  other arithmetic  6.94 us (5%)
    pallas_call x1, Pallas kernels, shards(): pl.pallas_call(conv_kernel, out_shape=[bricks, bricks], in_specs=[smem] +...  24.1 us
    ppermute x10, starting transfers between devices, total_over(): value = mine + lax.ppermute(other, axis, pairs)  20.2 us
    ppermute x4, starting transfers between devices, with_halo(): before = lax.ppermute(last, axis, up)  15.4 us
    ppermute x10, waiting for transfers between devices, total_over(): other = lax.ppermute(value, axis, pairs)  11.1 us
    ppermute x10, starting transfers between devices, total_over(): other = lax.ppermute(value, axis, pairs)  10.8 us
    pallas_call x1, Pallas kernels, shards(): pl.pallas_call(functools.partial(wgrad_kernel, scale), out_shape=jax.Shap...  10.6 us
    ppermute x10, waiting for transfers between devices, total_over(): value = mine + lax.ppermute(other, axis, pairs)  8.55 us
    pallas_call x1, Pallas kernels, shards(): pl.pallas_call(place_kernel, out_shape=[jax.ShapeDtypeStruct(grid_shape,...  6.81 us
  transfers between devices with their start and end apart: 28, of which 11 were waited for; matrix products, arithmetic and copies ran while one was open for 10% of the time, Pallas kernels for 18%

profile of v2, /device:TPU:0, one launch (start us, length us, event | category | flops | bytes accessed | tf_op | source)
XLA Modules:
  0.0 134.0 jit_solution(8225355854873847890)
XLA Ops:
  0.6 6.8 %place.1 = (bf16[2,32,128,128]{3,2,1,0:T(8,128)(2,1)}, bf16[2,32,128,128]{3,2,1,0:T(8,128)(2,1)}, bf16[8,512,128]{2,1,0:T(8,128)(2,1)}) custom-call(s32[8]{0:T(128)} %pos_ref.5, s32[8,512]{1,0:T(8,128)} %occ_ref.3, bf16[8,512,128]{2,1,0:T(8,128)(2,1)} %feat_ref.1, bf16[8,512,128]{2,1,0:T(8,128)(2,1)} %cot_ref.1), custom_call_target="tpu_custom_call" | custom-call | tf_op jit(solution)/shard_map/place/pallas_call | solution.py:179
  7.4 0.9 fusion.3
  8.3 4.8 %collective-permute-start = (bf16[2,1,128,128]{3,2,1,0:T(8,128)(2,1)S(1)}, bf16[2,1,128,128]{3,2,1,0:T(8,128)(2,1)S(1)}, u32[]{:S(2)}, u32[]{:S(2)}) collective-permute-start(bf16[2,1,128,128]{3,2,1,0:T(8,128)(2,1)S(1)} %get-tuple-element.20), channel_id=1, source_target_pairs={{0,4},{4,8},{8,12},{12,16},{16,20},{20,24},{24,28},{1,5},{5,9},{9,... | collective-permute-start | bytes 196616 | tf_op jit(solution)/shard_map/ppermute | solution.py:124
  13.1 1.3 collective-permute-start.1
  14.4 0.9 fusion.2
  15.3 4.5 %collective-permute-start.4 = (bf16[2,1,128,128]{3,2,1,0:T(8,128)(2,1)S(1)}, bf16[2,1,128,128]{3,2,1,0:T(8,128)(2,1)S(1)}, u32[]{:S(2)}, u32[]{:S(2)}) collective-permute-start(bf16[2,1,128,128]{3,2,1,0:T(8,128)(2,1)S(1)} %get-tuple-element.18), channel_id=1, source_target_pairs={{0,4},{4,8},{8,12},{12,16},{16,20},{20,24},{24,28},{1,5},{5,9},{9,... | collective-permute-start | bytes 196616 | tf_op jit(solution)/shard_map/ppermute | solution.py:124
  19.8 1.3 collective-permute-start.5
  21.2 2.1 %constant_dynamic-update-slice_fusion.1 = bf16[2,34,128,128]{3,2,1,0:T(8,128)(2,1)S(1)} fusion(bf16[2,34,128,128]{3,2,1,0:T(8,128)(2,1)S(1)} %constant_dynamic-update-slice_fusion.2, bf16[2,32,128,128]{3,2,1,0:T(8,128)(2,1)} %get-tuple-element.8), kind=kLoop, calls=%fused_computation.42 | loop fusion | bytes 4194304
  23.4 1.3 collective-permute-start.3
  24.7 3.0 %collective-permute-start.2 = (bf16[2,34,8,128]{3,2,1,0:T(8,128)(2,1)S(1)}, bf16[2,34,8,128]{3,2,1,0:T(8,128)(2,1)S(1)}, u32[]{:S(2)}, u32[]{:S(2)}) collective-permute-start(bf16[2,34,8,128]{3,2,1,0:T(8,128)(2,1)S(1)} %get-tuple-element.15), channel_id=1, source_target_pairs={{0,1},{1,2},{2,3},{4,5},{5,6},{6,7},{8,9},{9,10},{10,11},{12,13},{... | collective-permute-start | bytes 417800 | tf_op jit(solution)/shard_map/ppermute | solution.py:124
  27.8 0.6 constant_dynamic-update-slice_fusion.5
  28.4 1.7 %constant_dynamic-update-slice_fusion.4 = bf16[2,34,128,128]{3,2,1,0:T(8,128)(2,1)} fusion(bf16[2,34,128,128]{3,2,1,0:T(8,128)(2,1)} %constant_dynamic-update-slice_fusion.5, bf16[2,32,128,128]{3,2,1,0:T(8,128)(2,1)S(1)} %copy-done.2), kind=kLoop, calls=%fused_computation.45 | loop fusion | bytes 4194304
  30.1 0.6 constant_dynamic-update-slice_fusion.3
  30.7 1.7 %pad_maximum_fusion.gx_ref = bf16[2,34,144,128]{3,2,1,0:T(8,128)(2,1)} fusion(bf16[2,34,8,128]{3,2,1,0:T(8,128)(2,1)S(1)} %collective-permute-done.3, bf16[2,34,128,128]{3,2,1,0:T(8,128)(2,1)S(1)} %constant_dynamic-update-slice_fusion, bf16[2,34,8,128]{3,2,1,0:T(8,128)(2,1)S(1)} %collective-permute-done.2), kind=kLoop, calls=%fused_computation | loop fusion | flops 7520256 | bytes 5013504 | tf_op jit(solution)/shard_map/concatenate | solution.py:126
  32.4 10.6 %wgrad.1 = f32[3,128,1152]{2,1,0:T(8,128)} custom-call(s32[8]{0:T(128)} %pos_ref.5, bf16[2,34,144,128]{3,2,1,0:T(8,128)(2,1)} %pad_maximum_fusion.gx_ref, bf16[8,512,128]{2,1,0:T(8,128)(2,1)} %get-tuple-element.12.mc_ref), custom_call_target="tpu_custom_call" | custom-call | tf_op jit(solution)/shard_map/wgrad/pallas_call | solution.py:190
  43.0 2.2 %copy.10 = f32[3,128,1152]{1,2,0:T(8,128)S(1)} copy(f32[3,128,1152]{2,1,0:T(8,128)} %wgrad.1) | data formatting | bytes 3538944 | tf_op jit(solution)/shard_map/wgrad/pallas_call | solution.py:190
  45.3 0.9 copy-done
  46.3 1.2 collective-permute-start.18
  47.5 1.0 fusion
  48.5 1.3 collective-permute-start.7
  49.8 3.0 %collective-permute-start.6 = (bf16[2,34,8,128]{3,2,1,0:T(8,128)(2,1)S(1)}, bf16[2,34,8,128]{3,2,1,0:T(8,128)(2,1)S(1)}, u32[]{:S(2)}, u32[]{:S(2)}) collective-permute-start(bf16[2,34,8,128]{3,2,1,0:T(8,128)(2,1)S(1)} %get-tuple-element.13), channel_id=1, source_target_pairs={{0,1},{1,2},{2,3},{4,5},{5,6},{6,7},{8,9},{9,10},{10,11},{12,13},{... | collective-permute-start | bytes 417800 | tf_op jit(solution)/shard_map/ppermute | solution.py:124
  53.1 1.6 %copy.9 = bf16[27,128,128]{2,1,0:T(8,128)(2,1)} copy(bf16[27,128,128]{1,2,0:T(8,128)(2,1)S(1)} %reverse_bitcast_fusion) | data formatting | bytes 1769472 | tf_op jit(solution)/shard_map/transpose | solution.py:205
  54.8 1.3 collective-permute-start.8
  56.1 3.3 %pad_maximum_fusion.1.gd_ref = bf16[2,34,144,128]{3,2,1,0:T(8,128)(2,1)} fusion(bf16[2,34,8,128]{3,2,1,0:T(8,128)(2,1)S(1)} %collective-permute-done.7, bf16[2,34,128,128]{3,2,1,0:T(8,128)(2,1)} %constant_dynamic-update-slice_fusion.3, bf16[2,34,8,128]{3,2,1,0:T(8,128)(2,1)S(1)} %collective-permute-done.6), kind=kLoop, calls=%fused_computation.1 | loop fusion | flops 7520256 | bytes 5013504 | tf_op jit(solution)/shard_map/concatenate | solution.py:126
  59.6 3.1 %collective-permute-start.19 = (f32[448,128]{1,0:T(8,128)S(1)}, f32[448,128]{1,0:T(8,128)S(1)}, u32[]{:S(2)}, u32[]{:S(2)}) collective-permute-start(f32[448,128]{1,0:T(8,128)S(1)} %constant_dynamic-slice_fusion.3), channel_id=1, source_target_pairs={{0,4},{4,0},{8,12},{12,8},{16,20},{20,16},{24,28},{28,24},{1,5},{5... | collective-permute-start | bytes 688136 | tf_op jit(solution)/shard_map/ppermute | solution.py:139
  62.8 2.4 %collective-permute-start.9 = (f32[448,128]{1,0:T(8,128)S(1)}, f32[448,128]{1,0:T(8,128)S(1)}, u32[]{:S(2)}, u32[]{:S(2)}) collective-permute-start(f32[448,128]{1,0:T(8,128)S(1)} %constant_dynamic-slice_fusion.8), channel_id=1, source_target_pairs={{0,2},{1,3},{2,0},{3,1},{4,6},{5,7},{6,4},{7,5},{8,10},{9,11},{10,... | collective-permute-start | bytes 688136 | tf_op jit(solution)/shard_map/ppermute | solution.py:139
  65.2 3.4 %collective-permute-done.19 = f32[448,128]{1,0:T(8,128)S(1)} collective-permute-done((f32[448,128]{1,0:T(8,128)S(1)}, f32[448,128]{1,0:T(8,128)S(1)}, u32[]{:S(2)}, u32[]{:S(2)}) %collective-permute-start.19) | collective-permute-done | bytes 229408 | tf_op jit(solution)/shard_map/ppermute | solution.py:139
  68.6 3.2 %collective-permute-start.20 = (f32[224,128]{1,0:T(8,128)S(1)}, f32[224,128]{1,0:T(8,128)S(1)}, u32[]{:S(2)}, u32[]{:S(2)}) collective-permute-start(f32[224,128]{1,0:T(8,128)S(1)} %constant_dynamic-slice_fusion.2), channel_id=1, source_target_pairs={{0,8},{4,12},{8,0},{12,4},{16,24},{20,28},{24,16},{28,20},{1,9},{5... | collective-permute-start | bytes 344072 | tf_op jit(solution)/shard_map/ppermute | solution.py:139
  72.2 2.4 %collective-permute-done.20 = f32[224,128]{1,0:T(8,128)S(1)} collective-permute-done((f32[224,128]{1,0:T(8,128)S(1)}, f32[224,128]{1,0:T(8,128)S(1)}, u32[]{:S(2)}, u32[]{:S(2)}) %collective-permute-start.20) | collective-permute-done | bytes 114720 | tf_op jit(solution)/shard_map/ppermute | solution.py:139
  74.6 3.2 %collective-permute-start.21 = (f32[112,128]{1,0:T(8,128)S(1)}, f32[112,128]{1,0:T(8,128)S(1)}, u32[]{:S(2)}, u32[]{:S(2)}) collective-permute-start(f32[112,128]{1,0:T(8,128)S(1)} %constant_dynamic-slice_fusion.1), channel_id=1, source_target_pairs={{0,16},{4,20},{8,24},{12,28},{16,0},{20,4},{24,8},{28,12},{1,17},{... | collective-permute-start | bytes 172040 | tf_op jit(solution)/shard_map/ppermute | solution.py:139
  77.9 1.5 %collective-permute-start.11 = (f32[112,128]{1,0:T(8,128)S(1)}, f32[112,128]{1,0:T(8,128)S(1)}, u32[]{:S(2)}, u32[]{:S(2)}) collective-permute-start(f32[112,128]{1,0:T(8,128)S(1)} %constant_dynamic-slice_fusion.6), channel_id=1, source_target_pairs={{0,8},{4,12},{8,0},{12,4},{16,24},{20,28},{24,16},{28,20},{1,9},{5... | collective-permute-start | bytes 172040 | tf_op jit(solution)/shard_map/ppermute | solution.py:139
  80.0 1.5 %collective-permute-start.22 = (f32[56,128]{1,0:T(8,128)S(1)}, f32[56,128]{1,0:T(8,128)S(1)}, u32[]{:S(2)}, u32[]{:S(2)}) collective-permute-start(f32[56,128]{1,0:T(8,128)S(1)} %constant_dynamic-slice_fusion), channel_id=1, source_target_pairs={{0,2},{1,3},{2,0},{3,1},{4,6},{5,7},{6,4},{7,5},{8,10},{9,11},{10,... | collective-permute-start | bytes 86024 | tf_op jit(solution)/shard_map/ppermute | solution.py:139
  81.5 0.6 collective-permute-done.11
  82.1 2.4 %collective-permute-start.12 = (f32[56,128]{1,0:T(8,128)S(1)}, f32[56,128]{1,0:T(8,128)S(1)}, u32[]{:S(2)}, u32[]{:S(2)}) collective-permute-start(f32[56,128]{1,0:T(8,128)S(1)} %constant_dynamic-slice_fusion.5), channel_id=1, source_target_pairs={{0,16},{4,20},{8,24},{12,28},{16,0},{20,4},{24,8},{28,12},{1,17},{... | collective-permute-start | bytes 86024 | tf_op jit(solution)/shard_map/ppermute | solution.py:139
  84.5 0.8 collective-permute-start.23
  85.4 1.6 %collective-permute-done.12 = f32[56,128]{1,0:T(8,128)S(1)} collective-permute-done((f32[56,128]{1,0:T(8,128)S(1)}, f32[56,128]{1,0:T(8,128)S(1)}, u32[]{:S(2)}, u32[]{:S(2)}) %collective-permute-start.12) | collective-permute-done | bytes 28704 | tf_op jit(solution)/shard_map/ppermute | solution.py:139
  87.0 2.3 %collective-permute-start.13 = (f32[56,128]{1,0:T(8,128)S(1)}, f32[56,128]{1,0:T(8,128)S(1)}, u32[]{:S(2)}, u32[]{:S(2)}) collective-permute-start(f32[56,128]{1,0:T(8,128)S(1)} %dynamic-slice_add_fusion.9), channel_id=1, source_target_pairs={{0,16},{4,20},{8,24},{12,28},{16,0},{20,4},{24,8},{28,12},{1,17},{... | collective-permute-start | bytes 86024 | tf_op jit(solution)/shard_map/ppermute | solution.py:142
  89.3 1.6 %collective-permute-start.24 = (f32[112,128]{1,0:T(8,128)S(1)}, f32[112,128]{1,0:T(8,128)S(1)}, u32[]{:S(2)}, u32[]{:S(2)}) collective-permute-start(f32[112,128]{1,0:T(8,128)S(1)} %pad_maximum_fusion.12), channel_id=1, source_target_pairs={{0,16},{4,20},{8,24},{12,28},{16,0},{20,4},{24,8},{28,12},{1,17},{... | collective-permute-start | bytes 172040 | tf_op jit(solution)/shard_map/ppermute | solution.py:142
  90.9 1.0 collective-permute-done.13
  91.9 2.3 %collective-permute-start.14 = (f32[112,128]{1,0:T(8,128)S(1)}, f32[112,128]{1,0:T(8,128)S(1)}, u32[]{:S(2)}, u32[]{:S(2)}) collective-permute-start(f32[112,128]{1,0:T(8,128)S(1)} %pad_maximum_fusion.11), channel_id=1, source_target_pairs={{0,8},{4,12},{8,0},{12,4},{16,24},{20,28},{24,16},{28,20},{1,9},{5... | collective-permute-start | bytes 172040 | tf_op jit(solution)/shard_map/ppermute | solution.py:142
  94.5 2.8 %collective-permute-start.25 = (f32[224,128]{1,0:T(8,128)S(1)}, f32[224,128]{1,0:T(8,128)S(1)}, u32[]{:S(2)}, u32[]{:S(2)}) collective-permute-start(f32[224,128]{1,0:T(8,128)S(1)} %pad_maximum_fusion.10), channel_id=1, source_target_pairs={{0,8},{4,12},{8,0},{12,4},{16,24},{20,28},{24,16},{28,20},{1,9},{5... | collective-permute-start | bytes 344072 | tf_op jit(solution)/shard_map/ppermute | solution.py:142
  97.4 2.7 %collective-permute-done.25 = f32[224,128]{1,0:T(8,128)S(1)} collective-permute-done((f32[224,128]{1,0:T(8,128)S(1)}, f32[224,128]{1,0:T(8,128)S(1)}, u32[]{:S(2)}, u32[]{:S(2)}) %collective-permute-start.25) | collective-permute-done | bytes 114720 | tf_op jit(solution)/shard_map/ppermute | solution.py:142
  100.2 2.0 %collective-permute-done.15 = f32[224,128]{1,0:T(8,128)S(1)} collective-permute-done((f32[224,128]{1,0:T(8,128)S(1)}, f32[224,128]{1,0:T(8,128)S(1)}, u32[]{:S(2)}, u32[]{:S(2)}) %collective-permute-start.15) | collective-permute-done | bytes 114720 | tf_op jit(solution)/shard_map/ppermute | solution.py:142
  102.2 0.8 collective-permute-start.16
  103.0 3.2 %collective-permute-done.26 = f32[448,128]{1,0:T(8,128)S(1)} collective-permute-done((f32[448,128]{1,0:T(8,128)S(1)}, f32[448,128]{1,0:T(8,128)S(1)}, u32[]{:S(2)}, u32[]{:S(2)}) %collective-permute-start.26) | collective-permute-done | bytes 229408 | tf_op jit(solution)/shard_map/ppermute | solution.py:142
  106.3 2.0 %collective-permute-done.16 = f32[448,128]{1,0:T(8,128)S(1)} collective-permute-done((f32[448,128]{1,0:T(8,128)S(1)}, f32[448,128]{1,0:T(8,128)S(1)}, u32[]{:S(2)}, u32[]{:S(2)}) %collective-permute-start.16) | collective-permute-done | bytes 229408 | tf_op jit(solution)/shard_map/ppermute | solution.py:142
  108.4 24.1 %conv.1 = (bf16[8,512,128]{2,1,0:T(8,128)(2,1)}, bf16[8,512,128]{2,1,0:T(8,128)(2,1)}) custom-call(s32[8]{0:T(128)} %pos_ref.5, s32[8,512]{1,0:T(8,128)} %occ_ref.3, bf16[2,34,144,128]{3,2,1,0:T(8,128)(2,1)} %pad_maximum_fusion.gx_ref, bf16[2,34,144,128]{3,2,1,0:T(8,128)(2,1)} %pad_maximum_fusion.1.gd_ref, bf16[3,1152,128]{2,1,0:T(8,128)(2,1)} %bitcast.12, ...), custom_call_target="tpu_custom_call" | custom-call | flops 7247757312 | bytes 8388608 | tf_op jit(solution)/shard_map/conv/pallas_call | solution.py:206
  132.7 1.3 pad_maximum_fusion.2
  (74 shorter events, 2.7 us)
Async XLA Ops:
  8.3 12.8 %collective-permute-start = (bf16[2,1,128,128]{3,2,1,0:T(8,128)(2,1)S(1)}, bf16[2,1,128,128]{3,2,1,0:T(8,128)(2,1)S(1)}, u32[]{:S(2)}, u32[]{:S(2)}) collective-permute-start(bf16[2,1,128,128]{3,2,1,0:T(8,128)(2,1)S(1)} %get-tuple-element.20), channel_id=1, source_target_pairs={{0,4},{4,8},{8,12},{12,16},{16,20},{20,24},{24,28},{1,5},{5,9},{9,... | collective-permute-start | bytes 196616 | tf_op jit(solution)/shard_map/ppermute | solution.py:124
  13.1 10.2 %collective-permute-start.1 = (bf16[2,1,128,128]{3,2,1,0:T(8,128)(2,1)S(1)}, bf16[2,1,128,128]{3,2,1,0:T(8,128)(2,1)S(1)}, u32[]{:S(2)}, u32[]{:S(2)}) collective-permute-start(bf16[2,1,128,128]{3,2,1,0:T(8,128)(2,1)S(1)} %get-tuple-element.19), channel_id=1, source_target_pairs={{4,0},{8,4},{12,8},{16,12},{20,16},{24,20},{28,24},{5,1},{9,5},{13... | collective-permute-start | bytes 196616 | tf_op jit(solution)/shard_map/ppermute | solution.py:125
  15.3 12.5 %collective-permute-start.4 = (bf16[2,1,128,128]{3,2,1,0:T(8,128)(2,1)S(1)}, bf16[2,1,128,128]{3,2,1,0:T(8,128)(2,1)S(1)}, u32[]{:S(2)}, u32[]{:S(2)}) collective-permute-start(bf16[2,1,128,128]{3,2,1,0:T(8,128)(2,1)S(1)} %get-tuple-element.18), channel_id=1, source_target_pairs={{0,4},{4,8},{8,12},{12,16},{16,20},{20,24},{24,28},{1,5},{5,9},{9,... | collective-permute-start | bytes 196616 | tf_op jit(solution)/shard_map/ppermute | solution.py:124
  19.8 10.2 %collective-permute-start.5 = (bf16[2,1,128,128]{3,2,1,0:T(8,128)(2,1)S(1)}, bf16[2,1,128,128]{3,2,1,0:T(8,128)(2,1)S(1)}, u32[]{:S(2)}, u32[]{:S(2)}) collective-permute-start(bf16[2,1,128,128]{3,2,1,0:T(8,128)(2,1)S(1)} %get-tuple-element.17), channel_id=1, source_target_pairs={{4,0},{8,4},{12,8},{16,12},{20,16},{24,20},{28,24},{5,1},{9,5},{13... | collective-permute-start | bytes 196616 | tf_op jit(solution)/shard_map/ppermute | solution.py:125
  21.2 7.2 %copy-start.2 = (bf16[2,32,128,128]{3,2,1,0:T(8,128)(2,1)S(1)}, bf16[2,32,128,128]{3,2,1,0:T(8,128)(2,1)}, u32[]{:S(2)}) copy-start(bf16[2,32,128,128]{3,2,1,0:T(8,128)(2,1)} %get-tuple-element.9) | copy-start | bytes 6291460
  23.4 7.3 %collective-permute-start.3 = (bf16[2,34,8,128]{3,2,1,0:T(8,128)(2,1)S(1)}, bf16[2,34,8,128]{3,2,1,0:T(8,128)(2,1)S(1)}, u32[]{:S(2)}, u32[]{:S(2)}) collective-permute-start(bf16[2,34,8,128]{3,2,1,0:T(8,128)(2,1)S(1)} %get-tuple-element.16), channel_id=1, source_target_pairs={{1,0},{2,1},{3,2},{5,4},{6,5},{7,6},{9,8},{10,9},{11,10},{13,12},{... | collective-permute-start | bytes 417800 | tf_op jit(solution)/shard_map/ppermute | solution.py:125
  24.7 6.0 %collective-permute-start.2 = (bf16[2,34,8,128]{3,2,1,0:T(8,128)(2,1)S(1)}, bf16[2,34,8,128]{3,2,1,0:T(8,128)(2,1)S(1)}, u32[]{:S(2)}, u32[]{:S(2)}) collective-permute-start(bf16[2,34,8,128]{3,2,1,0:T(8,128)(2,1)S(1)} %get-tuple-element.15), channel_id=1, source_target_pairs={{0,1},{1,2},{2,3},{4,5},{5,6},{6,7},{8,9},{9,10},{10,11},{12,13},{... | collective-permute-start | bytes 417800 | tf_op jit(solution)/shard_map/ppermute | solution.py:124
  45.2 7.7 %copy-start.3 = (bf16[27,128,128]{2,1,0:T(8,128)(2,1)S(1)}, bf16[27,128,128]{2,1,0:T(8,128)(2,1)}, u32[]{:S(2)}) copy-start(bf16[27,128,128]{2,1,0:T(8,128)(2,1)} %param.6) | copy-start | bytes 2654212
  45.3 0.9 copy-start
  46.3 13.2 %collective-permute-start.18 = (f32[896,128]{1,0:T(8,128)S(1)}, f32[896,128]{1,0:T(8,128)S(1)}, u32[]{:S(2)}, u32[]{:S(2)}) collective-permute-start(f32[896,128]{1,0:T(8,128)S(1)} %constant_dynamic-slice_fusion.4), channel_id=1, source_target_pairs={{0,1},{1,0},{2,3},{3,2},{4,5},{5,4},{6,7},{7,6},{8,9},{9,8},{10,11... | collective-permute-start | bytes 1376264 | tf_op jit(solution)/shard_map/ppermute | solution.py:139
  48.5 7.6 %collective-permute-start.7 = (bf16[2,34,8,128]{3,2,1,0:T(8,128)(2,1)S(1)}, bf16[2,34,8,128]{3,2,1,0:T(8,128)(2,1)S(1)}, u32[]{:S(2)}, u32[]{:S(2)}) collective-permute-start(bf16[2,34,8,128]{3,2,1,0:T(8,128)(2,1)S(1)} %get-tuple-element.14), channel_id=1, source_target_pairs={{1,0},{2,1},{3,2},{5,4},{6,5},{7,6},{9,8},{10,9},{11,10},{13,12},{... | collective-permute-start | bytes 417800 | tf_op jit(solution)/shard_map/ppermute | solution.py:125
  49.8 6.3 %collective-permute-start.6 = (bf16[2,34,8,128]{3,2,1,0:T(8,128)(2,1)S(1)}, bf16[2,34,8,128]{3,2,1,0:T(8,128)(2,1)S(1)}, u32[]{:S(2)}, u32[]{:S(2)}) collective-permute-start(bf16[2,34,8,128]{3,2,1,0:T(8,128)(2,1)S(1)} %get-tuple-element.13), channel_id=1, source_target_pairs={{0,1},{1,2},{2,3},{4,5},{5,6},{6,7},{8,9},{9,10},{10,11},{12,13},{... | collective-permute-start | bytes 417800 | tf_op jit(solution)/shard_map/ppermute | solution.py:124
  54.8 4.7 %copy-start.1 = (f32[1792,128]{1,0:T(8,128)S(1)}, f32[1792,128]{1,0:T(8,128)}, u32[]{:S(2)}) copy-start(f32[1792,128]{1,0:T(8,128)} %copy-done) | copy-start | bytes 2752516
  54.8 7.9 %collective-permute-start.8 = (f32[896,128]{1,0:T(8,128)S(1)}, f32[896,128]{1,0:T(8,128)S(1)}, u32[]{:S(2)}, u32[]{:S(2)}) collective-permute-start(f32[896,128]{1,0:T(8,128)S(1)} %constant_dynamic-slice_fusion.9), channel_id=1, source_target_pairs={{0,1},{1,0},{2,3},{3,2},{4,5},{5,4},{6,7},{7,6},{8,9},{9,8},{10,11... | collective-permute-start | bytes 1376264 | tf_op jit(solution)/shard_map/ppermute | solution.py:139
  59.6 9.0 %collective-permute-start.19 = (f32[448,128]{1,0:T(8,128)S(1)}, f32[448,128]{1,0:T(8,128)S(1)}, u32[]{:S(2)}, u32[]{:S(2)}) collective-permute-start(f32[448,128]{1,0:T(8,128)S(1)} %constant_dynamic-slice_fusion.3), channel_id=1, source_target_pairs={{0,4},{4,0},{8,12},{12,8},{16,20},{20,16},{24,28},{28,24},{1,5},{5... | collective-permute-start | bytes 688136 | tf_op jit(solution)/shard_map/ppermute | solution.py:139
  62.8 9.1 %collective-permute-start.9 = (f32[448,128]{1,0:T(8,128)S(1)}, f32[448,128]{1,0:T(8,128)S(1)}, u32[]{:S(2)}, u32[]{:S(2)}) collective-permute-start(f32[448,128]{1,0:T(8,128)S(1)} %constant_dynamic-slice_fusion.8), channel_id=1, source_target_pairs={{0,2},{1,3},{2,0},{3,1},{4,6},{5,7},{6,4},{7,5},{8,10},{9,11},{10,... | collective-permute-start | bytes 688136 | tf_op jit(solution)/shard_map/ppermute | solution.py:139
  68.6 6.0 %collective-permute-start.20 = (f32[224,128]{1,0:T(8,128)S(1)}, f32[224,128]{1,0:T(8,128)S(1)}, u32[]{:S(2)}, u32[]{:S(2)}) collective-permute-start(f32[224,128]{1,0:T(8,128)S(1)} %constant_dynamic-slice_fusion.2), channel_id=1, source_target_pairs={{0,8},{4,12},{8,0},{12,4},{16,24},{20,28},{24,16},{28,20},{1,9},{5... | collective-permute-start | bytes 344072 | tf_op jit(solution)/shard_map/ppermute | solution.py:139
  71.9 5.9 %collective-permute-start.10 = (f32[224,128]{1,0:T(8,128)S(1)}, f32[224,128]{1,0:T(8,128)S(1)}, u32[]{:S(2)}, u32[]{:S(2)}) collective-permute-start(f32[224,128]{1,0:T(8,128)S(1)} %constant_dynamic-slice_fusion.7), channel_id=1, source_target_pairs={{0,4},{4,0},{8,12},{12,8},{16,20},{20,16},{24,28},{28,24},{1,5},{5... | collective-permute-start | bytes 344072 | tf_op jit(solution)/shard_map/ppermute | solution.py:139
  74.6 5.3 %collective-permute-start.21 = (f32[112,128]{1,0:T(8,128)S(1)}, f32[112,128]{1,0:T(8,128)S(1)}, u32[]{:S(2)}, u32[]{:S(2)}) collective-permute-start(f32[112,128]{1,0:T(8,128)S(1)} %constant_dynamic-slice_fusion.1), channel_id=1, source_target_pairs={{0,16},{4,20},{8,24},{12,28},{16,0},{20,4},{24,8},{28,12},{1,17},{... | collective-permute-start | bytes 172040 | tf_op jit(solution)/shard_map/ppermute | solution.py:139
  77.9 4.2 %collective-permute-start.11 = (f32[112,128]{1,0:T(8,128)S(1)}, f32[112,128]{1,0:T(8,128)S(1)}, u32[]{:S(2)}, u32[]{:S(2)}) collective-permute-start(f32[112,128]{1,0:T(8,128)S(1)} %constant_dynamic-slice_fusion.6), channel_id=1, source_target_pairs={{0,8},{4,12},{8,0},{12,4},{16,24},{20,28},{24,16},{28,20},{1,9},{5... | collective-permute-start | bytes 172040 | tf_op jit(solution)/shard_map/ppermute | solution.py:139
  80.0 4.5 %collective-permute-start.22 = (f32[56,128]{1,0:T(8,128)S(1)}, f32[56,128]{1,0:T(8,128)S(1)}, u32[]{:S(2)}, u32[]{:S(2)}) collective-permute-start(f32[56,128]{1,0:T(8,128)S(1)} %constant_dynamic-slice_fusion), channel_id=1, source_target_pairs={{0,2},{1,3},{2,0},{3,1},{4,6},{5,7},{6,4},{7,5},{8,10},{9,11},{10,... | collective-permute-start | bytes 86024 | tf_op jit(solution)/shard_map/ppermute | solution.py:139
  82.1 4.8 %collective-permute-start.12 = (f32[56,128]{1,0:T(8,128)S(1)}, f32[56,128]{1,0:T(8,128)S(1)}, u32[]{:S(2)}, u32[]{:S(2)}) collective-permute-start(f32[56,128]{1,0:T(8,128)S(1)} %constant_dynamic-slice_fusion.5), channel_id=1, source_target_pairs={{0,16},{4,20},{8,24},{12,28},{16,0},{20,4},{24,8},{28,12},{1,17},{... | collective-permute-start | bytes 86024 | tf_op jit(solution)/shard_map/ppermute | solution.py:139
  84.5 4.8 %collective-permute-start.23 = (f32[56,128]{1,0:T(8,128)S(1)}, f32[56,128]{1,0:T(8,128)S(1)}, u32[]{:S(2)}, u32[]{:S(2)}) collective-permute-start(f32[56,128]{1,0:T(8,128)S(1)} %dynamic-slice_add_fusion.8), channel_id=1, source_target_pairs={{0,2},{1,3},{2,0},{3,1},{4,6},{5,7},{6,4},{7,5},{8,10},{9,11},{10,... | collective-permute-start | bytes 86024 | tf_op jit(solution)/shard_map/ppermute | solution.py:142
  87.0 4.9 %collective-permute-start.13 = (f32[56,128]{1,0:T(8,128)S(1)}, f32[56,128]{1,0:T(8,128)S(1)}, u32[]{:S(2)}, u32[]{:S(2)}) collective-permute-start(f32[56,128]{1,0:T(8,128)S(1)} %dynamic-slice_add_fusion.9), channel_id=1, source_target_pairs={{0,16},{4,20},{8,24},{12,28},{16,0},{20,4},{24,8},{28,12},{1,17},{... | collective-permute-start | bytes 86024 | tf_op jit(solution)/shard_map/ppermute | solution.py:142
  89.3 5.1 %collective-permute-start.24 = (f32[112,128]{1,0:T(8,128)S(1)}, f32[112,128]{1,0:T(8,128)S(1)}, u32[]{:S(2)}, u32[]{:S(2)}) collective-permute-start(f32[112,128]{1,0:T(8,128)S(1)} %pad_maximum_fusion.12), channel_id=1, source_target_pairs={{0,16},{4,20},{8,24},{12,28},{16,0},{20,4},{24,8},{28,12},{1,17},{... | collective-permute-start | bytes 172040 | tf_op jit(solution)/shard_map/ppermute | solution.py:142
  91.9 5.4 %collective-permute-start.14 = (f32[112,128]{1,0:T(8,128)S(1)}, f32[112,128]{1,0:T(8,128)S(1)}, u32[]{:S(2)}, u32[]{:S(2)}) collective-permute-start(f32[112,128]{1,0:T(8,128)S(1)} %pad_maximum_fusion.11), channel_id=1, source_target_pairs={{0,8},{4,12},{8,0},{12,4},{16,24},{20,28},{24,16},{28,20},{1,9},{5... | collective-permute-start | bytes 172040 | tf_op jit(solution)/shard_map/ppermute | solution.py:142
  94.5 5.5 %collective-permute-start.25 = (f32[224,128]{1,0:T(8,128)S(1)}, f32[224,128]{1,0:T(8,128)S(1)}, u32[]{:S(2)}, u32[]{:S(2)}) collective-permute-start(f32[224,128]{1,0:T(8,128)S(1)} %pad_maximum_fusion.10), channel_id=1, source_target_pairs={{0,8},{4,12},{8,0},{12,4},{16,24},{20,28},{24,16},{28,20},{1,9},{5... | collective-permute-start | bytes 344072 | tf_op jit(solution)/shard_map/ppermute | solution.py:142
  97.3 4.9 %collective-permute-start.15 = (f32[224,128]{1,0:T(8,128)S(1)}, f32[224,128]{1,0:T(8,128)S(1)}, u32[]{:S(2)}, u32[]{:S(2)}) collective-permute-start(f32[224,128]{1,0:T(8,128)S(1)} %pad_maximum_fusion.9), channel_id=1, source_target_pairs={{0,4},{4,0},{8,12},{12,8},{16,20},{20,16},{24,28},{28,24},{1,5},{5... | collective-permute-start | bytes 344072 | tf_op jit(solution)/shard_map/ppermute | solution.py:142
  100.1 6.1 %collective-permute-start.26 = (f32[448,128]{1,0:T(8,128)S(1)}, f32[448,128]{1,0:T(8,128)S(1)}, u32[]{:S(2)}, u32[]{:S(2)}) collective-permute-start(f32[448,128]{1,0:T(8,128)S(1)} %pad_maximum_fusion.8), channel_id=1, source_target_pairs={{0,4},{4,0},{8,12},{12,8},{16,20},{20,16},{24,28},{28,24},{1,5},{5... | collective-permute-start | bytes 688136 | tf_op jit(solution)/shard_map/ppermute | solution.py:142
  102.2 6.1 %collective-permute-start.16 = (f32[448,128]{1,0:T(8,128)S(1)}, f32[448,128]{1,0:T(8,128)S(1)}, u32[]{:S(2)}, u32[]{:S(2)}) collective-permute-start(f32[448,128]{1,0:T(8,128)S(1)} %pad_maximum_fusion.7), channel_id=1, source_target_pairs={{0,2},{1,3},{2,0},{3,1},{4,6},{5,7},{6,4},{7,5},{8,10},{9,11},{10,... | collective-permute-start | bytes 688136 | tf_op jit(solution)/shard_map/ppermute | solution.py:142
  106.2 26.3 %collective-permute-start.27 = (f32[896,128]{1,0:T(8,128)S(1)}, f32[896,128]{1,0:T(8,128)S(1)}, u32[]{:S(2)}, u32[]{:S(2)}) collective-permute-start(f32[896,128]{1,0:T(8,128)S(1)} %pad_maximum_fusion.6), channel_id=1, source_target_pairs={{0,1},{1,0},{2,3},{3,2},{4,5},{5,4},{6,7},{7,6},{8,9},{9,8},{10,11... | collective-permute-start | bytes 1376264 | tf_op jit(solution)/shard_map/ppermute | solution.py:142
  108.4 24.3 %collective-permute-start.17 = (f32[896,128]{1,0:T(8,128)S(1)}, f32[896,128]{1,0:T(8,128)S(1)}, u32[]{:S(2)}, u32[]{:S(2)}) collective-permute-start(f32[896,128]{1,0:T(8,128)S(1)} %pad_maximum_fusion.5), channel_id=1, source_target_pairs={{0,1},{1,0},{2,3},{3,2},{4,5},{5,4},{6,7},{7,6},{8,9},{9,8},{10,11... | collective-permute-start | bytes 1376264 | tf_op jit(solution)/shard_map/ppermute | solution.py:142

commit v3 on v1

--- a/solution.py
+++ b/solution.py
@@ -29,9 +29,8 @@
     return over_rows(on, chosen.astype(F32))
 
 
-def place_kernel(pos_ref, occ_ref, feat_ref, cot_ref, gx_ref, gd_ref, mc_ref):
-    for grid in (gx_ref, gd_ref):
-        grid[...] = jnp.zeros_like(grid)
+def place_kernel(pos_ref, occ_ref, feat_ref, cot_ref, grids_ref, mc_ref):
+    grids_ref[...] = jnp.zeros_like(grids_ref)
 
     @pl.loop(0, feat_ref.shape[0])
     def _(slot):
@@ -48,8 +47,8 @@
             bz = at % REGION_Z
             rows = pl.ds(pl.multiple_of(by * FACE, FACE), FACE)
             for a in range(BRICK):
-                gx_ref[bz, bx * BRICK + a, rows, :] = mx[a * FACE : (a + 1) * FACE]
-                gd_ref[bz, bx * BRICK + a, rows, :] = mc[a * FACE : (a + 1) * FACE]
+                grids_ref[bz, bx * BRICK + a, rows, :] = mx[a * FACE : (a + 1) * FACE]
+                grids_ref[REGION_Z + bz, bx * BRICK + a, rows, :] = mc[a * FACE : (a + 1) * FACE]
 
 
 def expand(at, wide, patches):
@@ -98,20 +97,19 @@
             out_ref[p] += over_rows(mc_ref[slot], part) * scale
 
 
-def conv_kernel(pos_ref, occ_ref, gx_ref, gd_ref, wf_ref, wb_ref, out_ref, gi_ref, wide, patches):
-    for grid, weight, result in ((gx_ref, wf_ref, out_ref), (gd_ref, wb_ref, gi_ref)):
-        widen(grid, wide)
-
-        @pl.loop(0, result.shape[0])
-        def _(slot):
-            at = pos_ref[slot]
-            expand(at, wide, patches)
-            keep = slot_mask(occ_ref, slot) * (at >= 0).astype(F32)
-            total = jnp.zeros((BRICK * FACE, 128), F32)
-            for p in range(3):
-                part = patches[p * FACE : p * FACE + BRICK * FACE]
-                total += jnp.dot(part, weight[p], preferred_element_type=F32)
-            result[slot] = jnp.where(keep > 0.5, total, 0.0).astype(BF16)
+def conv_kernel(pos_ref, occ_ref, grid_ref, weight_ref, result_ref, wide, patches):
+    widen(grid_ref, wide)
+
+    @pl.loop(0, result_ref.shape[0])
+    def _(slot):
+        at = pos_ref[slot]
+        expand(at, wide, patches)
+        keep = slot_mask(occ_ref, slot) * (at >= 0).astype(F32)
+        total = jnp.zeros((BRICK * FACE, 128), F32)
+        for p in range(3):
+            part = patches[p * FACE : p * FACE + BRICK * FACE]
+            total += jnp.dot(part, weight_ref[p], preferred_element_type=F32)
+        result_ref[slot] = jnp.where(keep > 0.5, total, 0.0).astype(BF16)
 
 
 def with_halo(value, sides):
@@ -127,6 +125,50 @@
     return value
 
 
+def halve(value, step):
+    axis, stride = step
+    pairs = [(i, i ^ stride) for i in range(lax.axis_size(axis))]
+    bit = (lax.axis_index(axis) // stride) % 2
+    half = value.shape[0] // 2
+    mine = lax.dynamic_slice_in_dim(value, bit * half, half, axis=0)
+    other = lax.dynamic_slice_in_dim(value, (1 - bit) * half, half, axis=0)
+    return mine, lax.ppermute(other, axis, pairs)
+
+
+def double(value, step):
+    axis, stride = step
+    pairs = [(i, i ^ stride) for i in range(lax.axis_size(axis))]
+    bit = (lax.axis_index(axis) // stride) % 2
+    other = lax.ppermute(value, axis, pairs)
+    low = jnp.where(bit == 0, value, other)
+    high = jnp.where(bit == 0, other, value)
+    return jnp.concatenate([low, high], axis=0)
+
+
+def axis_steps(axis):
+    return [(axis, 1 << k) for k in range(lax.axis_size(axis).bit_length() - 1)]
+
+
+def all_sum(value, beside):
+    rows = value.shape[0]
+    unit = 2 * 8 * lax.axis_size("gx") * lax.axis_size("gy")
+    padded = -(-rows // unit) * unit
+    value = jnp.pad(value, ((0, padded - rows), (0, 0)))
+    along_x, along_y = axis_steps("gx"), axis_steps("gy")
+    orders = (along_y + along_x, along_y[:1] + along_x + along_y[1:])
+    parts = [value[: padded // 2], value[padded // 2 :]]
+    made = list(beside)
+    for number, steps in enumerate(zip(*orders)):
+        pairs = [halve(part, step) for part, step in zip(parts, steps)]
+        if number < len(made):
+            a, b, made[number] = lax.optimization_barrier((pairs[0][0], pairs[1][0], made[number]))
+            pairs = [(a, pairs[0][1]), (b, pairs[1][1])]
+        parts = [mine + other for mine, other in pairs]
+    for steps in reversed(list(zip(*orders))):
+        parts = [double(part, step) for part, step in zip(parts, steps)]
+    return jnp.concatenate(parts, axis=0)[:rows], made
+
+
 def shards(features, weights, cotangent, occupancy, slot_pos):
     slots, voxels, channels = features.shape
     devices = lax.axis_size("gx") * lax.axis_size("gy")
@@ -134,7 +176,7 @@
     vmem = pl.BlockSpec(memory_space=pltpu.VMEM)
     smem = pl.BlockSpec(memory_space=pltpu.SMEM)
     params = pltpu.CompilerParams(vmem_limit_bytes=VMEM_LIMIT)
-    grid_shape = (REGION_Z, REGION_X * BRICK, REGION_Y * FACE, channels)
+    grid_shape = (2 * REGION_Z, REGION_X * BRICK, REGION_Y * FACE, channels)
     wide_shape = (REGION_Z, REGION_X * BRICK + 2, REGION_Y * FACE + 2 * BRICK, channels)
     scratch = [
         pltpu.VMEM(wide_shape, F32),
@@ -142,46 +184,53 @@
     ]
     bricks = jax.ShapeDtypeStruct(features.shape, BF16)
 
-    gx, gd, mc = pl.pallas_call(
+    grids, mc = pl.pallas_call(
         place_kernel,
-        out_shape=[jax.ShapeDtypeStruct(grid_shape, BF16)] * 2 + [bricks],
+        out_shape=[jax.ShapeDtypeStruct(grid_shape, BF16), bricks],
         in_specs=[smem, vmem, vmem, vmem],
-        out_specs=[vmem] * 3,
+        out_specs=[vmem] * 2,
         compiler_params=params,
         name="place",
     )(slot_pos, occupancy, features, cotangent)
-
-    sides = (("gx", 1, 1), ("gy", 2, BRICK))
-    gx = with_halo(gx, sides)
+    grids = with_halo(grids, (("gx", 1, 1), ("gy", 2, BRICK)))
+
+    def grid_spec(which):
+        return pl.BlockSpec(wide_shape, lambda i: (which, 0, 0, 0))
+
     local = pl.pallas_call(
         functools.partial(wgrad_kernel, scale),
+        grid=(1,),
         out_shape=jax.ShapeDtypeStruct((3, channels, 9 * channels), F32),
-        in_specs=[smem, vmem, vmem],
+        in_specs=[smem, grid_spec(0), vmem],
         out_specs=vmem,
         scratch_shapes=scratch,
         compiler_params=params,
         name="wgrad",
-    )(slot_pos, gx, mc)
-    summed = lax.psum(local, ("gx", "gy"))
-    grad_weight = (
-        summed.reshape(3, channels, 9, channels).transpose(0, 2, 3, 1).reshape(27, channels, channels)
-    )
-
-    gd = with_halo(gd, sides)
-    w_forward = weights.reshape(3, 9 * channels, channels)
+    )(slot_pos, grids, mc)
+    local = local.reshape(3, channels, 9, channels).transpose(0, 2, 3, 1)
+
+    def conv(which, weight, name):
+        return pl.pallas_call(
+            conv_kernel,
+            grid=(1,),
+            out_shape=bricks,
+            in_specs=[smem, vmem, grid_spec(which), vmem],
+            out_specs=vmem,
+            scratch_shapes=scratch,
+            compiler_params=params,
+            cost_estimate=pl.CostEstimate(
+                flops=2 * slots * voxels * 27 * channels * channels,
+                bytes_accessed=4 << 20,
+                transcendentals=0,
+            ),
+            name=name,
+        )(slot_pos, occupancy, grids, weight)
+
+    outputs = conv(0, weights.reshape(3, 9 * channels, channels), "forward")
     w_backward = weights[::-1].transpose(0, 2, 1).reshape(3, 9 * channels, channels)
-    outputs, grad_input = pl.pallas_call(
-        conv_kernel,
-        out_shape=[bricks, bricks],
-        in_specs=[smem] + [vmem] * 5,
-        out_specs=[vmem, vmem],
-        scratch_shapes=scratch,
-        compiler_params=params,
-        cost_estimate=pl.CostEstimate(
-            flops=4 * slots * voxels * 27 * channels * channels, bytes_accessed=8 << 20, transcendentals=0
-        ),
-        name="conv",
-    )(slot_pos, occupancy, gx, gd, w_forward, w_backward)
+    grad_input = conv(1, w_backward, "input_grad")
+    summed, (outputs, grad_input) = all_sum(local.reshape(27 * channels, channels), (outputs, grad_input))
+    grad_weight = summed.reshape(27, channels, channels)
     return (outputs, grad_input, grad_weight)
 
 

time: 203 us -> 123 us (0.61)
  waiting for transfers between devices: 110 us -> 27.2 us
  between operations: 14.2 us -> 1.17 us
  starting transfers between devices: 20.6 us -> 32.9 us
  other arithmetic: 3.42 us -> 7.31 us
  local copies, waits for them, and re-layouts: 13.5 us -> 10.7 us
    psum x1 -> x0, waiting for transfers between devices: 109 us -> none  [shards(): summed = lax.psum(local, ('gx', 'gy'))]
    ppermute x0 -> x20, waiting for transfers between devices: none -> 24.8 us  [the longest x10 15.1 us: double(): other = lax.ppermute(value, axis, pairs)]
    ppermute x0 -> x20, starting transfers between devices: none -> 22.3 us  [the longest x10 14.9 us: halve(): return (mine, lax.ppermute(other, axis, pairs))]
    ppermute x4 -> x2, starting transfers between devices: 15.4 us -> 8.01 us  [with_halo(): before = lax.ppermute(last, axis, up)]
    ppermute x4 -> x2, starting transfers between devices: 5.17 us -> 2.58 us  [with_halo(): after = lax.ppermute(leading, axis, down)]
    concatenate x2 -> x1, other arithmetic: 3.42 us -> 5.39 us  [with_halo(): value = jnp.concatenate([before, value, after], axis=dim)]
    pallas_call x2 -> x3, Pallas kernels: 34.7 us -> 36.6 us  [the longest x2 26 us: conv(): pl.pallas_call(conv_kernel, grid=(1,), out_shape=bricks, in_specs=[smem,...]
    unnamed x7 -> x6, local copies, waits for them, and re-layouts: 5.28 us -> 5.2 us
  transfers between devices with their start and end apart: 9 -> 24, of which waited for: 2 -> 16; matrix products, arithmetic and copies ran while one was open for 7% -> 5% of each run, Pallas kernels for 17% -> 21%
where the time goes in v3:
time: 123 us
  Pallas kernels  43.3 us (35%)
  starting transfers between devices  32.9 us (27%)
  waiting for transfers between devices  27.2 us (22%)
  local copies, waits for them, and re-layouts  10.7 us (9%)
  other arithmetic  7.31 us (6%)
    pallas_call x2, Pallas kernels, conv(): pl.pallas_call(conv_kernel, grid=(1,), out_shape=bricks, in_specs=[smem,...  26 us
    ppermute x10, waiting for transfers between devices, double(): other = lax.ppermute(value, axis, pairs)  15.1 us
    ppermute x10, starting transfers between devices, halve(): return (mine, lax.ppermute(other, axis, pairs))  14.9 us
    pallas_call x1, Pallas kernels, shards(): pl.pallas_call(functools.partial(wgrad_kernel, scale), grid=(1,), out_sha...  10.6 us
    ppermute x10, waiting for transfers between devices, halve(): return (mine, lax.ppermute(other, axis, pairs))  9.65 us
    ppermute x2, starting transfers between devices, with_halo(): before = lax.ppermute(last, axis, up)  8.01 us
    ppermute x10, starting transfers between devices, double(): other = lax.ppermute(value, axis, pairs)  7.39 us
    pallas_call x1, Pallas kernels, shards(): pl.pallas_call(place_kernel, out_shape=[jax.ShapeDtypeStruct(grid_shape,...  6.73 us
  transfers between devices with their start and end apart: 24, of which 16 were waited for; matrix products, arithmetic and copies ran while one was open for 5% of the time, Pallas kernels for 21%

profile of v3, /device:TPU:0, one launch (start us, length us, event | category | flops | bytes accessed | tf_op | source)
XLA Modules:
  0.0 122.5 jit_solution(7110315774629616287)
XLA Ops:
  0.6 6.7 %place.1 = (bf16[4,32,128,128]{3,2,1,0:T(8,128)(2,1)}, bf16[8,512,128]{2,1,0:T(8,128)(2,1)}) custom-call(s32[8]{0:T(128)} %pos_ref.7, s32[8,512]{1,0:T(8,128)} %occ_ref.5, bf16[8,512,128]{2,1,0:T(8,128)(2,1)} %feat_ref.1, bf16[8,512,128]{2,1,0:T(8,128)(2,1)} %cot_ref.1), custom_call_target="tpu_custom_call" | custom-call | tf_op jit(solution)/shard_map/place/pallas_call | solution.py:187
  7.4 1.0 fusion.1
  8.3 5.0 %collective-permute-start = (bf16[4,1,128,128]{3,2,1,0:T(8,128)(2,1)S(1)}, bf16[4,1,128,128]{3,2,1,0:T(8,128)(2,1)S(1)}, u32[]{:S(2)}, u32[]{:S(2)}) collective-permute-start(bf16[4,1,128,128]{3,2,1,0:T(8,128)(2,1)S(1)} %get-tuple-element.22), channel_id=1, source_target_pairs={{0,4},{4,8},{8,12},{12,16},{16,20},{20,24},{24,28},{1,5},{5,9},{9,... | collective-permute-start | bytes 393224 | tf_op jit(solution)/shard_map/ppermute | solution.py:122
  13.3 1.3 %collective-permute-start.1 = (bf16[4,1,128,128]{3,2,1,0:T(8,128)(2,1)S(1)}, bf16[4,1,128,128]{3,2,1,0:T(8,128)(2,1)S(1)}, u32[]{:S(2)}, u32[]{:S(2)}) collective-permute-start(bf16[4,1,128,128]{3,2,1,0:T(8,128)(2,1)S(1)} %get-tuple-element.21), channel_id=1, source_target_pairs={{4,0},{8,4},{12,8},{16,12},{20,16},{24,20},{28,24},{5,1},{9,5},{13... | collective-permute-start | bytes 393224 | tf_op jit(solution)/shard_map/ppermute | solution.py:123
  14.6 1.3 %collective-permute-done = bf16[4,1,128,128]{3,2,1,0:T(8,128)(2,1)S(1)} collective-permute-done((bf16[4,1,128,128]{3,2,1,0:T(8,128)(2,1)S(1)}, bf16[4,1,128,128]{3,2,1,0:T(8,128)(2,1)S(1)}, u32[]{:S(2)}, u32[]{:S(2)}) %collective-permute-start) | collective-permute-done | bytes 131104 | tf_op jit(solution)/shard_map/ppermute | solution.py:122
  16.0 3.1 %constant_dynamic-update-slice_fusion.1 = bf16[4,34,128,128]{3,2,1,0:T(8,128)(2,1)S(1)} fusion(bf16[4,34,128,128]{3,2,1,0:T(8,128)(2,1)S(1)} %constant_dynamic-update-slice_fusion.2, bf16[4,32,128,128]{3,2,1,0:T(8,128)(2,1)} %get-tuple-element.11), kind=kLoop, calls=%fused_computation.41 | loop fusion | bytes 8388608
  19.1 1.1 collective-permute-done.1
  20.2 2.1 %copy-done = bf16[4,34,128,128]{3,2,1,0:T(8,128)(2,1)} copy-done((bf16[4,34,128,128]{3,2,1,0:T(8,128)(2,1)}, bf16[4,34,128,128]{3,2,1,0:T(8,128)(2,1)S(1)}, u32[]{:S(2)}) %copy-start) | copy-done | bytes 4456472
  22.3 0.1 fusion
  22.4 1.3 %collective-permute-start.3 = (bf16[4,34,8,128]{3,2,1,0:T(8,128)(2,1)S(1)}, bf16[4,34,8,128]{3,2,1,0:T(8,128)(2,1)S(1)}, u32[]{:S(2)}, u32[]{:S(2)}) collective-permute-start(bf16[4,34,8,128]{3,2,1,0:T(8,128)(2,1)S(1)} %get-tuple-element.20), channel_id=1, source_target_pairs={{1,0},{2,1},{3,2},{5,4},{6,5},{7,6},{9,8},{10,9},{11,10},{13,12},{... | collective-permute-start | bytes 835592 | tf_op jit(solution)/shard_map/ppermute | solution.py:123
  23.7 3.0 %collective-permute-start.2 = (bf16[4,34,8,128]{3,2,1,0:T(8,128)(2,1)S(1)}, bf16[4,34,8,128]{3,2,1,0:T(8,128)(2,1)S(1)}, u32[]{:S(2)}, u32[]{:S(2)}) collective-permute-start(bf16[4,34,8,128]{3,2,1,0:T(8,128)(2,1)S(1)} %get-tuple-element.19), channel_id=1, source_target_pairs={{0,1},{1,2},{2,3},{4,5},{5,6},{6,7},{8,9},{9,10},{10,11},{12,13},{... | collective-permute-start | bytes 835592 | tf_op jit(solution)/shard_map/ppermute | solution.py:122
  27.0 1.7 %copy.10 = bf16[27,128,128]{2,1,0:T(8,128)(2,1)} copy(bf16[27,128,128]{1,2,0:T(8,128)(2,1)S(1)} %reverse_bitcast_fusion) | data formatting | bytes 1769472 | tf_op jit(solution)/shard_map/transpose | solution.py:230
  28.7 5.4 %pad_maximum_fusion.gx_ref.grid_ref = bf16[4,34,144,128]{3,2,1,0:T(8,128)(2,1)} fusion(bf16[4,34,8,128]{3,2,1,0:T(8,128)(2,1)S(1)} %collective-permute-done.3, bf16[4,34,128,128]{3,2,1,0:T(8,128)(2,1)} %copy-done, bf16[4,34,8,128]{3,2,1,0:T(8,128)(2,1)S(1)} %collective-permute-done.2), kind=kLoop, calls=%fused_computation | loop fusion | flops 15040512 | bytes 10027008 | tf_op jit(solution)/shard_map/concatenate | solution.py:124
  34.1 10.6 %wgrad.1 = f32[3,128,1152]{2,1,0:T(8,128)} custom-call(s32[8]{0:T(128)} %pos_ref.7, bf16[4,34,144,128]{3,2,1,0:T(8,128)(2,1)} %pad_maximum_fusion.gx_ref.grid_ref, bf16[8,512,128]{2,1,0:T(8,128)(2,1)} %get-tuple-element.12.mc_ref), custom_call_target="tpu_custom_call" | custom-call | tf_op jit(solution)/shard_map/wgrad/pallas_call | solution.py:200
  44.7 2.2 %copy.9 = f32[3,128,1152]{1,2,0:T(8,128)S(1)} copy(f32[3,128,1152]{2,1,0:T(8,128)} %wgrad.1) | data formatting | bytes 3538944 | tf_op jit(solution)/shard_map/wgrad/pallas_call | solution.py:200
  46.8 0.1 pad_slice_fusion
  47.1 2.7 %collective-permute-start.5 = (f32[896,128]{1,0:T(8,128)S(1)}, f32[896,128]{1,0:T(8,128)S(1)}, u32[]{:S(2)}, u32[]{:S(2)}) collective-permute-start(f32[896,128]{1,0:T(8,128)S(1)} %get-tuple-element.29), channel_id=1, source_target_pairs={{0,1},{1,0},{2,3},{3,2},{4,5},{5,4},{6,7},{7,6},{8,9},{9,8},{10,11... | collective-permute-start | bytes 1376264 | tf_op jit(solution)/shard_map/ppermute | solution.py:135
  49.8 0.1 collective-permute-start.4
  49.9 13.0 %forward.1 = bf16[8,512,128]{2,1,0:T(8,128)(2,1)} custom-call(s32[8]{0:T(128)} %pos_ref.7, s32[8,512]{1,0:T(8,128)} %occ_ref.5, bf16[4,34,144,128]{3,2,1,0:T(8,128)(2,1)} %pad_maximum_fusion.gx_ref.grid_ref, bf16[3,1152,128]{2,1,0:T(8,128)(2,1)} %bitcast.12), custom_call_target="tpu_custom_call" | custom-call | flops 3623878656 | bytes 4194304 | tf_op jit(solution)/shard_map/forward/pallas_call | solution.py:213
  63.0 2.5 %collective-permute-start.15 = (f32[448,128]{1,0:T(8,128)S(1)}, f32[448,128]{1,0:T(8,128)S(1)}, u32[]{:S(2)}, u32[]{:S(2)}) collective-permute-start(f32[448,128]{1,0:T(8,128)S(1)} %get-tuple-element.39), channel_id=1, source_target_pairs={{0,4},{4,0},{8,12},{12,8},{16,20},{20,16},{24,28},{28,24},{1,5},{5... | collective-permute-start | bytes 688136 | tf_op jit(solution)/shard_map/ppermute | solution.py:135
  65.6 2.9 %collective-permute-start.6 = (f32[448,128]{1,0:T(8,128)S(1)}, f32[448,128]{1,0:T(8,128)S(1)}, u32[]{:S(2)}, u32[]{:S(2)}) collective-permute-start(f32[448,128]{1,0:T(8,128)S(1)} %get-tuple-element.35), channel_id=1, source_target_pairs={{0,2},{1,3},{2,0},{3,1},{4,6},{5,7},{6,4},{7,5},{8,10},{9,11},{10,... | collective-permute-start | bytes 688136 | tf_op jit(solution)/shard_map/ppermute | solution.py:135
  68.6 13.0 %input_grad.1 = bf16[8,512,128]{2,1,0:T(8,128)(2,1)} custom-call(s32[8]{0:T(128)} %pos_ref.7, s32[8,512]{1,0:T(8,128)} %occ_ref.5, bf16[4,34,144,128]{3,2,1,0:T(8,128)(2,1)} %pad_maximum_fusion.gx_ref.grid_ref, bf16[3,1152,128]{2,1,0:T(8,128)(2,1)} %bitcast.13), custom_call_target="tpu_custom_call" | custom-call | flops 3623878656 | bytes 4194304 | tf_op jit(solution)/shard_map/input_grad/pallas_call | solution.py:213
  81.6 1.6 %collective-permute-start.16 = (f32[224,128]{1,0:T(8,128)S(1)}, f32[224,128]{1,0:T(8,128)S(1)}, u32[]{:S(2)}, u32[]{:S(2)}) collective-permute-start(f32[224,128]{1,0:T(8,128)S(1)} %constant_dynamic-slice_fusion.2), channel_id=1, source_target_pairs={{0,8},{4,12},{8,0},{12,4},{16,24},{20,28},{24,16},{28,20},{1,9},{5... | collective-permute-start | bytes 344072 | tf_op jit(solution)/shard_map/ppermute | solution.py:135
  83.3 0.7 collective-permute-start.7
  84.0 2.5 %collective-permute-done.16 = f32[224,128]{1,0:T(8,128)S(1)} collective-permute-done((f32[224,128]{1,0:T(8,128)S(1)}, f32[224,128]{1,0:T(8,128)S(1)}, u32[]{:S(2)}, u32[]{:S(2)}) %collective-permute-start.16) | collective-permute-done | bytes 114720 | tf_op jit(solution)/shard_map/ppermute | solution.py:135
  86.5 2.6 %collective-permute-start.17 = (f32[112,128]{1,0:T(8,128)S(1)}, f32[112,128]{1,0:T(8,128)S(1)}, u32[]{:S(2)}, u32[]{:S(2)}) collective-permute-start(f32[112,128]{1,0:T(8,128)S(1)} %constant_dynamic-slice_fusion.1), channel_id=1, source_target_pairs={{0,16},{4,20},{8,24},{12,28},{16,0},{20,4},{24,8},{28,12},{1,17},{... | collective-permute-start | bytes 172040 | tf_op jit(solution)/shard_map/ppermute | solution.py:135
  89.2 0.7 collective-permute-start.8
  89.9 1.8 %collective-permute-done.17 = f32[112,128]{1,0:T(8,128)S(1)} collective-permute-done((f32[112,128]{1,0:T(8,128)S(1)}, f32[112,128]{1,0:T(8,128)S(1)}, u32[]{:S(2)}, u32[]{:S(2)}) %collective-permute-start.17) | collective-permute-done | bytes 57376 | tf_op jit(solution)/shard_map/ppermute | solution.py:135
  91.7 0.1 collective-permute-start.18
  91.8 1.6 %collective-permute-done.8 = f32[112,128]{1,0:T(8,128)S(1)} collective-permute-done((f32[112,128]{1,0:T(8,128)S(1)}, f32[112,128]{1,0:T(8,128)S(1)}, u32[]{:S(2)}, u32[]{:S(2)}) %collective-permute-start.8) | collective-permute-done | bytes 57376 | tf_op jit(solution)/shard_map/ppermute | solution.py:135
  93.5 1.0 collective-permute-start.9
  94.5 1.2 collective-permute-done.18
  95.7 0.9 collective-permute-start.19
  96.5 2.5 %collective-permute-done.9 = f32[56,128]{1,0:T(8,128)S(1)} collective-permute-done((f32[56,128]{1,0:T(8,128)S(1)}, f32[56,128]{1,0:T(8,128)S(1)}, u32[]{:S(2)}, u32[]{:S(2)}) %collective-permute-start.9) | collective-permute-done | bytes 28704 | tf_op jit(solution)/shard_map/ppermute | solution.py:135
  99.0 0.5 collective-permute-start.10
  99.6 2.6 %collective-permute-start.20 = (f32[112,128]{1,0:T(8,128)S(1)}, f32[112,128]{1,0:T(8,128)S(1)}, u32[]{:S(2)}, u32[]{:S(2)}) collective-permute-start(f32[112,128]{1,0:T(8,128)S(1)} %pad_maximum_fusion.11), channel_id=1, source_target_pairs={{0,16},{4,20},{8,24},{12,28},{16,0},{20,4},{24,8},{28,12},{1,17},{... | collective-permute-start | bytes 172040 | tf_op jit(solution)/shard_map/ppermute | solution.py:142
  102.2 1.7 %collective-permute-done.10 = f32[56,128]{1,0:T(8,128)S(1)} collective-permute-done((f32[56,128]{1,0:T(8,128)S(1)}, f32[56,128]{1,0:T(8,128)S(1)}, u32[]{:S(2)}, u32[]{:S(2)}) %collective-permute-start.10) | collective-permute-done | bytes 28704 | tf_op jit(solution)/shard_map/ppermute | solution.py:142
  103.9 0.1 collective-permute-start.11
  104.0 0.7 collective-permute-done.20
  104.7 1.7 %collective-permute-start.21 = (f32[224,128]{1,0:T(8,128)S(1)}, f32[224,128]{1,0:T(8,128)S(1)}, u32[]{:S(2)}, u32[]{:S(2)}) collective-permute-start(f32[224,128]{1,0:T(8,128)S(1)} %pad_maximum_fusion.9), channel_id=1, source_target_pairs={{0,8},{4,12},{8,0},{12,4},{16,24},{20,28},{24,16},{28,20},{1,9},{5... | collective-permute-start | bytes 344072 | tf_op jit(solution)/shard_map/ppermute | solution.py:142
  106.4 1.8 %collective-permute-done.11 = f32[112,128]{1,0:T(8,128)S(1)} collective-permute-done((f32[112,128]{1,0:T(8,128)S(1)}, f32[112,128]{1,0:T(8,128)S(1)}, u32[]{:S(2)}, u32[]{:S(2)}) %collective-permute-start.11) | collective-permute-done | bytes 57376 | tf_op jit(solution)/shard_map/ppermute | solution.py:142
  108.3 1.3 %collective-permute-done.21 = f32[224,128]{1,0:T(8,128)S(1)} collective-permute-done((f32[224,128]{1,0:T(8,128)S(1)}, f32[224,128]{1,0:T(8,128)S(1)}, u32[]{:S(2)}, u32[]{:S(2)}) %collective-permute-start.21) | collective-permute-done | bytes 114720 | tf_op jit(solution)/shard_map/ppermute | solution.py:142
  109.6 1.4 %collective-permute-start.22 = (f32[448,128]{1,0:T(8,128)S(1)}, f32[448,128]{1,0:T(8,128)S(1)}, u32[]{:S(2)}, u32[]{:S(2)}) collective-permute-start(f32[448,128]{1,0:T(8,128)S(1)} %pad_maximum_fusion.7), channel_id=1, source_target_pairs={{0,4},{4,0},{8,12},{12,8},{16,20},{20,16},{24,28},{28,24},{1,5},{5... | collective-permute-start | bytes 688136 | tf_op jit(solution)/shard_map/ppermute | solution.py:142
  111.0 2.0 %collective-permute-done.12 = f32[224,128]{1,0:T(8,128)S(1)} collective-permute-done((f32[224,128]{1,0:T(8,128)S(1)}, f32[224,128]{1,0:T(8,128)S(1)}, u32[]{:S(2)}, u32[]{:S(2)}) %collective-permute-start.12) | collective-permute-done | bytes 114720 | tf_op jit(solution)/shard_map/ppermute | solution.py:142
  113.2 2.5 %collective-permute-done.22 = f32[448,128]{1,0:T(8,128)S(1)} collective-permute-done((f32[448,128]{1,0:T(8,128)S(1)}, f32[448,128]{1,0:T(8,128)S(1)}, u32[]{:S(2)}, u32[]{:S(2)}) %collective-permute-start.22) | collective-permute-done | bytes 229408 | tf_op jit(solution)/shard_map/ppermute | solution.py:142
  115.9 3.3 %collective-permute-done.13 = f32[448,128]{1,0:T(8,128)S(1)} collective-permute-done((f32[448,128]{1,0:T(8,128)S(1)}, f32[448,128]{1,0:T(8,128)S(1)}, u32[]{:S(2)}, u32[]{:S(2)}) %collective-permute-start.13) | collective-permute-done | bytes 229408 | tf_op jit(solution)/shard_map/ppermute | solution.py:142
  119.4 1.7 %collective-permute-done.14 = f32[896,128]{1,0:T(8,128)S(1)} collective-permute-done((f32[896,128]{1,0:T(8,128)S(1)}, f32[896,128]{1,0:T(8,128)S(1)}, u32[]{:S(2)}, u32[]{:S(2)}) %collective-permute-start.14) | collective-permute-done | bytes 458784 | tf_op jit(solution)/shard_map/ppermute | solution.py:142
  121.2 1.3 %pad_maximum_fusion.1 = f32[3456,128]{1,0:T(8,128)} fusion(f32[896,128]{1,0:T(8,128)S(1)} %get-tuple-element.28, f32[896,128]{1,0:T(8,128)S(1)} %get-tuple-element.27, f32[896,128]{1,0:T(8,128)S(1)} %get-tuple-element.26, f32[896,128]{1,0:T(8,128)S(1)} %get-tuple-element.25), kind=kLoop, calls=%fused_computation.2 | loop fusion | flops 1327104 | bytes 3604480 | tf_op jit(solution)/shard_map/concatenate | solution.py:169
  (57 shorter events, 1.4 us)
Async XLA Ops:
  8.3 7.6 %collective-permute-start = (bf16[4,1,128,128]{3,2,1,0:T(8,128)(2,1)S(1)}, bf16[4,1,128,128]{3,2,1,0:T(8,128)(2,1)S(1)}, u32[]{:S(2)}, u32[]{:S(2)}) collective-permute-start(bf16[4,1,128,128]{3,2,1,0:T(8,128)(2,1)S(1)} %get-tuple-element.22), channel_id=1, source_target_pairs={{0,4},{4,8},{8,12},{12,16},{16,20},{20,24},{24,28},{1,5},{5,9},{9,... | collective-permute-start | bytes 393224 | tf_op jit(solution)/shard_map/ppermute | solution.py:122
  13.3 6.9 %collective-permute-start.1 = (bf16[4,1,128,128]{3,2,1,0:T(8,128)(2,1)S(1)}, bf16[4,1,128,128]{3,2,1,0:T(8,128)(2,1)S(1)}, u32[]{:S(2)}, u32[]{:S(2)}) collective-permute-start(bf16[4,1,128,128]{3,2,1,0:T(8,128)(2,1)S(1)} %get-tuple-element.21), channel_id=1, source_target_pairs={{4,0},{8,4},{12,8},{16,12},{20,16},{24,20},{28,24},{5,1},{9,5},{13... | collective-permute-start | bytes 393224 | tf_op jit(solution)/shard_map/ppermute | solution.py:123
  16.0 11.0 %copy-start.1 = (bf16[27,128,128]{2,1,0:T(8,128)(2,1)S(1)}, bf16[27,128,128]{2,1,0:T(8,128)(2,1)}, u32[]{:S(2)}) copy-start(bf16[27,128,128]{2,1,0:T(8,128)(2,1)} %param.6) | copy-start | bytes 2654212
  20.2 2.1 %copy-start = (bf16[4,34,128,128]{3,2,1,0:T(8,128)(2,1)}, bf16[4,34,128,128]{3,2,1,0:T(8,128)(2,1)S(1)}, u32[]{:S(2)}) copy-start(bf16[4,34,128,128]{3,2,1,0:T(8,128)(2,1)S(1)} %constant_dynamic-update-slice_fusion) | copy-start | bytes 13369348
  22.4 6.3 %collective-permute-start.3 = (bf16[4,34,8,128]{3,2,1,0:T(8,128)(2,1)S(1)}, bf16[4,34,8,128]{3,2,1,0:T(8,128)(2,1)S(1)}, u32[]{:S(2)}, u32[]{:S(2)}) collective-permute-start(bf16[4,34,8,128]{3,2,1,0:T(8,128)(2,1)S(1)} %get-tuple-element.20), channel_id=1, source_target_pairs={{1,0},{2,1},{3,2},{5,4},{6,5},{7,6},{9,8},{10,9},{11,10},{13,12},{... | collective-permute-start | bytes 835592 | tf_op jit(solution)/shard_map/ppermute | solution.py:123
  23.7 5.0 %collective-permute-start.2 = (bf16[4,34,8,128]{3,2,1,0:T(8,128)(2,1)S(1)}, bf16[4,34,8,128]{3,2,1,0:T(8,128)(2,1)S(1)}, u32[]{:S(2)}, u32[]{:S(2)}) collective-permute-start(bf16[4,34,8,128]{3,2,1,0:T(8,128)(2,1)S(1)} %get-tuple-element.19), channel_id=1, source_target_pairs={{0,1},{1,2},{2,3},{4,5},{5,6},{6,7},{8,9},{9,10},{10,11},{12,13},{... | collective-permute-start | bytes 835592 | tf_op jit(solution)/shard_map/ppermute | solution.py:122
  47.1 15.9 %collective-permute-start.5 = (f32[896,128]{1,0:T(8,128)S(1)}, f32[896,128]{1,0:T(8,128)S(1)}, u32[]{:S(2)}, u32[]{:S(2)}) collective-permute-start(f32[896,128]{1,0:T(8,128)S(1)} %get-tuple-element.29), channel_id=1, source_target_pairs={{0,1},{1,0},{2,3},{3,2},{4,5},{5,4},{6,7},{7,6},{8,9},{9,8},{10,11... | collective-permute-start | bytes 1376264 | tf_op jit(solution)/shard_map/ppermute | solution.py:135
  49.8 15.7 %collective-permute-start.4 = (f32[896,128]{1,0:T(8,128)S(1)}, f32[896,128]{1,0:T(8,128)S(1)}, u32[]{:S(2)}, u32[]{:S(2)}) collective-permute-start(f32[896,128]{1,0:T(8,128)S(1)} %get-tuple-element.31), channel_id=1, source_target_pairs={{0,1},{1,0},{2,3},{3,2},{4,5},{5,4},{6,7},{7,6},{8,9},{9,8},{10,11... | collective-permute-start | bytes 1376264 | tf_op jit(solution)/shard_map/ppermute | solution.py:135
  63.0 18.6 %collective-permute-start.15 = (f32[448,128]{1,0:T(8,128)S(1)}, f32[448,128]{1,0:T(8,128)S(1)}, u32[]{:S(2)}, u32[]{:S(2)}) collective-permute-start(f32[448,128]{1,0:T(8,128)S(1)} %get-tuple-element.39), channel_id=1, source_target_pairs={{0,4},{4,0},{8,12},{12,8},{16,20},{20,16},{24,28},{28,24},{1,5},{5... | collective-permute-start | bytes 688136 | tf_op jit(solution)/shard_map/ppermute | solution.py:135
  65.6 17.6 %collective-permute-start.6 = (f32[448,128]{1,0:T(8,128)S(1)}, f32[448,128]{1,0:T(8,128)S(1)}, u32[]{:S(2)}, u32[]{:S(2)}) collective-permute-start(f32[448,128]{1,0:T(8,128)S(1)} %get-tuple-element.35), channel_id=1, source_target_pairs={{0,2},{1,3},{2,0},{3,1},{4,6},{5,7},{6,4},{7,5},{8,10},{9,11},{10,... | collective-permute-start | bytes 688136 | tf_op jit(solution)/shard_map/ppermute | solution.py:135
  81.6 4.9 %collective-permute-start.16 = (f32[224,128]{1,0:T(8,128)S(1)}, f32[224,128]{1,0:T(8,128)S(1)}, u32[]{:S(2)}, u32[]{:S(2)}) collective-permute-start(f32[224,128]{1,0:T(8,128)S(1)} %constant_dynamic-slice_fusion.2), channel_id=1, source_target_pairs={{0,8},{4,12},{8,0},{12,4},{16,24},{20,28},{24,16},{28,20},{1,9},{5... | collective-permute-start | bytes 344072 | tf_op jit(solution)/shard_map/ppermute | solution.py:135
  83.3 5.9 %collective-permute-start.7 = (f32[224,128]{1,0:T(8,128)S(1)}, f32[224,128]{1,0:T(8,128)S(1)}, u32[]{:S(2)}, u32[]{:S(2)}) collective-permute-start(f32[224,128]{1,0:T(8,128)S(1)} %constant_dynamic-slice_fusion.6), channel_id=1, source_target_pairs={{0,4},{4,0},{8,12},{12,8},{16,20},{20,16},{24,28},{28,24},{1,5},{5... | collective-permute-start | bytes 344072 | tf_op jit(solution)/shard_map/ppermute | solution.py:135
  86.5 5.1 %collective-permute-start.17 = (f32[112,128]{1,0:T(8,128)S(1)}, f32[112,128]{1,0:T(8,128)S(1)}, u32[]{:S(2)}, u32[]{:S(2)}) collective-permute-start(f32[112,128]{1,0:T(8,128)S(1)} %constant_dynamic-slice_fusion.1), channel_id=1, source_target_pairs={{0,16},{4,20},{8,24},{12,28},{16,0},{20,4},{24,8},{28,12},{1,17},{... | collective-permute-start | bytes 172040 | tf_op jit(solution)/shard_map/ppermute | solution.py:135
  89.2 4.2 %collective-permute-start.8 = (f32[112,128]{1,0:T(8,128)S(1)}, f32[112,128]{1,0:T(8,128)S(1)}, u32[]{:S(2)}, u32[]{:S(2)}) collective-permute-start(f32[112,128]{1,0:T(8,128)S(1)} %constant_dynamic-slice_fusion.5), channel_id=1, source_target_pairs={{0,8},{4,12},{8,0},{12,4},{16,24},{20,28},{24,16},{28,20},{1,9},{5... | collective-permute-start | bytes 172040 | tf_op jit(solution)/shard_map/ppermute | solution.py:135
  91.7 3.9 %collective-permute-start.18 = (f32[56,128]{1,0:T(8,128)S(1)}, f32[56,128]{1,0:T(8,128)S(1)}, u32[]{:S(2)}, u32[]{:S(2)}) collective-permute-start(f32[56,128]{1,0:T(8,128)S(1)} %constant_dynamic-slice_fusion), channel_id=1, source_target_pairs={{0,2},{1,3},{2,0},{3,1},{4,6},{5,7},{6,4},{7,5},{8,10},{9,11},{10,... | collective-permute-start | bytes 86024 | tf_op jit(solution)/shard_map/ppermute | solution.py:135
  93.5 5.5 %collective-permute-start.9 = (f32[56,128]{1,0:T(8,128)S(1)}, f32[56,128]{1,0:T(8,128)S(1)}, u32[]{:S(2)}, u32[]{:S(2)}) collective-permute-start(f32[56,128]{1,0:T(8,128)S(1)} %constant_dynamic-slice_fusion.4), channel_id=1, source_target_pairs={{0,16},{4,20},{8,24},{12,28},{16,0},{20,4},{24,8},{28,12},{1,17},{... | collective-permute-start | bytes 86024 | tf_op jit(solution)/shard_map/ppermute | solution.py:135
  95.7 3.9 %collective-permute-start.19 = (f32[56,128]{1,0:T(8,128)S(1)}, f32[56,128]{1,0:T(8,128)S(1)}, u32[]{:S(2)}, u32[]{:S(2)}) collective-permute-start(f32[56,128]{1,0:T(8,128)S(1)} %dynamic-slice_add_fusion.4), channel_id=1, source_target_pairs={{0,2},{1,3},{2,0},{3,1},{4,6},{5,7},{6,4},{7,5},{8,10},{9,11},{10,... | collective-permute-start | bytes 86024 | tf_op jit(solution)/shard_map/ppermute | solution.py:142
  99.0 4.9 %collective-permute-start.10 = (f32[56,128]{1,0:T(8,128)S(1)}, f32[56,128]{1,0:T(8,128)S(1)}, u32[]{:S(2)}, u32[]{:S(2)}) collective-permute-start(f32[56,128]{1,0:T(8,128)S(1)} %dynamic-slice_add_fusion.5), channel_id=1, source_target_pairs={{0,16},{4,20},{8,24},{12,28},{16,0},{20,4},{24,8},{28,12},{1,17},{... | collective-permute-start | bytes 86024 | tf_op jit(solution)/shard_map/ppermute | solution.py:142
  99.6 5.1 %collective-permute-start.20 = (f32[112,128]{1,0:T(8,128)S(1)}, f32[112,128]{1,0:T(8,128)S(1)}, u32[]{:S(2)}, u32[]{:S(2)}) collective-permute-start(f32[112,128]{1,0:T(8,128)S(1)} %pad_maximum_fusion.11), channel_id=1, source_target_pairs={{0,16},{4,20},{8,24},{12,28},{16,0},{20,4},{24,8},{28,12},{1,17},{... | collective-permute-start | bytes 172040 | tf_op jit(solution)/shard_map/ppermute | solution.py:142
  103.9 4.2 %collective-permute-start.11 = (f32[112,128]{1,0:T(8,128)S(1)}, f32[112,128]{1,0:T(8,128)S(1)}, u32[]{:S(2)}, u32[]{:S(2)}) collective-permute-start(f32[112,128]{1,0:T(8,128)S(1)} %pad_maximum_fusion.10), channel_id=1, source_target_pairs={{0,8},{4,12},{8,0},{12,4},{16,24},{20,28},{24,16},{28,20},{1,9},{5... | collective-permute-start | bytes 172040 | tf_op jit(solution)/shard_map/ppermute | solution.py:142
  104.7 4.9 %collective-permute-start.21 = (f32[224,128]{1,0:T(8,128)S(1)}, f32[224,128]{1,0:T(8,128)S(1)}, u32[]{:S(2)}, u32[]{:S(2)}) collective-permute-start(f32[224,128]{1,0:T(8,128)S(1)} %pad_maximum_fusion.9), channel_id=1, source_target_pairs={{0,8},{4,12},{8,0},{12,4},{16,24},{20,28},{24,16},{28,20},{1,9},{5... | collective-permute-start | bytes 344072 | tf_op jit(solution)/shard_map/ppermute | solution.py:142
  108.2 4.9 %collective-permute-start.12 = (f32[224,128]{1,0:T(8,128)S(1)}, f32[224,128]{1,0:T(8,128)S(1)}, u32[]{:S(2)}, u32[]{:S(2)}) collective-permute-start(f32[224,128]{1,0:T(8,128)S(1)} %pad_maximum_fusion.8), channel_id=1, source_target_pairs={{0,4},{4,0},{8,12},{12,8},{16,20},{20,16},{24,28},{28,24},{1,5},{5... | collective-permute-start | bytes 344072 | tf_op jit(solution)/shard_map/ppermute | solution.py:142
  109.6 6.1 %collective-permute-start.22 = (f32[448,128]{1,0:T(8,128)S(1)}, f32[448,128]{1,0:T(8,128)S(1)}, u32[]{:S(2)}, u32[]{:S(2)}) collective-permute-start(f32[448,128]{1,0:T(8,128)S(1)} %pad_maximum_fusion.7), channel_id=1, source_target_pairs={{0,4},{4,0},{8,12},{12,8},{16,20},{20,16},{24,28},{28,24},{1,5},{5... | collective-permute-start | bytes 688136 | tf_op jit(solution)/shard_map/ppermute | solution.py:142
  113.1 6.1 %collective-permute-start.13 = (f32[448,128]{1,0:T(8,128)S(1)}, f32[448,128]{1,0:T(8,128)S(1)}, u32[]{:S(2)}, u32[]{:S(2)}) collective-permute-start(f32[448,128]{1,0:T(8,128)S(1)} %pad_maximum_fusion.6), channel_id=1, source_target_pairs={{0,2},{1,3},{2,0},{3,1},{4,6},{5,7},{6,4},{7,5},{8,10},{9,11},{10,... | collective-permute-start | bytes 688136 | tf_op jit(solution)/shard_map/ppermute | solution.py:142
  115.8 3.5 %collective-permute-start.23 = (f32[896,128]{1,0:T(8,128)S(1)}, f32[896,128]{1,0:T(8,128)S(1)}, u32[]{:S(2)}, u32[]{:S(2)}) collective-permute-start(f32[896,128]{1,0:T(8,128)S(1)} %pad_maximum_fusion.5), channel_id=1, source_target_pairs={{0,1},{1,0},{2,3},{3,2},{4,5},{5,4},{6,7},{7,6},{8,9},{9,8},{10,11... | collective-permute-start | bytes 1376264 | tf_op jit(solution)/shard_map/ppermute | solution.py:142
  119.3 1.9 %collective-permute-start.14 = (f32[896,128]{1,0:T(8,128)S(1)}, f32[896,128]{1,0:T(8,128)S(1)}, u32[]{:S(2)}, u32[]{:S(2)}) collective-permute-start(f32[896,128]{1,0:T(8,128)S(1)} %pad_maximum_fusion.4), channel_id=1, source_target_pairs={{0,1},{1,0},{2,3},{3,2},{4,5},{5,4},{6,7},{7,6},{8,9},{9,8},{10,11... | collective-permute-start | bytes 1376264 | tf_op jit(solution)/shard_map/ppermute | solution.py:142
